TPU v7x, 512 devices: a whole 4x8x8 slice. The times are simulated.
512 devices in a mesh: req: 32 (over x, y), sp: 16 (over z, core).
Axes of the slice: x: 4, y: 8, z: 8, core: 2. Of those that a mesh axis runs over, the one named last changes fastest.
Arguments:
- tokens: bfloat16 [23040, 64], P(('req', 'sp')), parts along dimension 0, may hold values from -6 to 6
- strip_rows: int32 [16], replicated, may hold values from 1 to 9, 90 in all
- first_filter: bfloat16 [3, 3, 3, 16, 384], replicated, may hold values from -0.3125 to 0.3125
- first_bias: float32 [384], replicated, may hold values from -3 to 3
- norm_gain: float32 [384], replicated, may hold values from 0.25 to 1.75
- second_filter: bfloat16 [3, 3, 3, 384, 384], P(None, None, None, None, 'sp'), may hold values from -0.0625 to 0.0625
- second_bias: float32 [384], replicated, may hold values from -3 to 3
Outputs:
- strips: bfloat16 [512, 2, 9, 16, 384], P(('req', 'sp')), parts along dimension 0
There are 32 independent parts, one for each index of `req`. A program takes and returns all parts, laid end to end along the dimension named above; an argument that names none is the same for every part. Nothing has to cross between parts.
Inputs may be any that keep to these rules, and one draw needn't show every extreme that they name: `strip_rows`: the lengths sum to 90; the largest is exactly 9 in every draw.
All inputs are finite; a program needn't handle non-finite values.
Results may differ from a plain program's by a relative error of at most 0.0037.
Values may be sent and summed in bfloat16 or wider, within the bound.
A program may use at most 64 MiB of HBM per device.

v0:
```python
import jax
import jax.numpy as jnp
from jax import lax
from jax.sharding import PartitionSpec as P

C = 16
FR = 2
PH = 45
PW = 8


def for_sending(x):
    return jax.tree.map(lambda a: a.astype(jnp.bfloat16) if a.dtype == jnp.float32 else a, x)


def arrange(flat):
    grid = flat.reshape(FR, PH, PW, 2, 2, C)
    grid = jnp.transpose(grid, (0, 1, 3, 2, 4, 5))
    return grid.reshape(FR, 2 * PH, 2 * PW, C)


def causal_conv(field, filters):
    return lax.conv_general_dilated(
        field[None],
        filters,
        (1, 1, 1),
        [(2, 0), (0, 0), (1, 1)],
        dimension_numbers=("NDHWC", "DHWIO", "NDHWC"),
        preferred_element_type=jnp.float32,
    )[0]


def activate(first, norm_gain):
    scale = lax.rsqrt(jnp.mean(first * first, axis=-1, keepdims=True) + 1e-06)
    return jax.nn.silu(first * scale * norm_gain).astype(jnp.bfloat16)


def pad_rows(field):
    return jnp.pad(field, ((0, 0), (1, 1), (0, 0), (0, 0)))


def per_device(tokens, strip_rows, first_filter, first_bias, norm_gain, second_filter, second_bias):
    group_size = lax.axis_size("sp")
    position = lax.axis_index("sp")
    most_rows = (2 * PH + group_size - 1) // group_size * 3 // 2
    starts = jnp.cumsum(strip_rows) - strip_rows
    everything = lax.all_gather(tokens, "sp", axis=0, tiled=True)
    latent = arrange(everything)
    first = causal_conv(pad_rows(latent), first_filter) + first_bias
    hidden = activate(first, norm_gain)
    width = second_filter.shape[4]
    part_bias = lax.dynamic_slice_in_dim(second_bias, position * width, width, 0)
    final = (causal_conv(pad_rows(hidden), second_filter) + part_bias).astype(jnp.bfloat16)
    padded_final = jnp.pad(final, ((0, 0), (0, most_rows), (0, 0), (0, 0)))

    def place(start, count):
        piece = lax.dynamic_slice_in_dim(padded_final, start, most_rows, 1)
        keep = jnp.arange(most_rows, dtype=jnp.int32) < count
        return jnp.where(keep[None, :, None, None], piece, jnp.zeros_like(piece))

    outgoing = jax.vmap(place)(starts, strip_rows)
    return jax.tree.map(
        lambda part, own: part.astype(own.dtype),
        lax.all_to_all(for_sending(outgoing), "sp", split_axis=0, concat_axis=4, tiled=True),
        outgoing,
    )


def solution(mesh):
    in_specs = (P(("req", "sp"), None), P(), P(), P(), P(), P(None, None, None, None, "sp"), P())
    out_specs = P(("req", "sp"), None, None, None, None)
    return jax.shard_map(
        per_device, mesh=mesh, in_specs=in_specs, out_specs=out_specs, check_vma=False
    )
```

profile of v0, /device:TPU:1, one launch (start us, length us, event | category | flops | bytes accessed | tf_op | source)
XLA Modules:
  0.0 107.2 jit_solution(2461209330298854086)
XLA Ops:
  0.0 0.0 copy-start
  0.0 25.4 %all-gather = bf16[16,45,64]{2,1,0:T(8,128)(2,1)S(1)} all-gather(bf16[1,45,64]{2,1,0:T(8,128)(2,1)} %bitcast.51), channel_id=1, replica_groups=mesh['req'=32,'sp'=16] {'sp'}, dimensions={0}, use_global_device_ids=true | all-gather | bytes 97920 | tf_op jit(solution)/shard_map/all_gather | solution.py:47
  25.4 0.3 reshape.63
  25.7 0.0 copy-start.2
  25.7 0.0 copy-start.4
  25.7 0.5 copy.45
  26.2 0.1 pad_bitcast_fusion.1
  26.4 0.7 copy.61
  27.1 0.1 fusion.16
  27.2 1.1 %copy.47 = bf16[2,92,1,8,5,16]{5,3,4,1,0,2:T(8,128)(2,1)S(1)} copy(bf16[2,92,1,8,5,16]{1,5,4,3,2,0:T(8,128)(2,1)S(1)} %fusion.16) | data formatting | bytes 471040 | tf_op jit(solution)/shard_map/conv_general_dilated | solution.py:23
  28.3 0.0 copy-done.2
  28.4 0.0 copy-done.4
  28.4 6.0 %broadcast_select_fusion = f32[2,90,8,3,384]{4,2,3,1,0:T(8,128)} fusion(pred[8,3]{0,1:T(4,128)(4,1)S(1)} %copy-done.4, bf16[3,3,3,16,384]{4,3,2,1,0:T(8,128)(2,1)S(1)} %copy-done.2, bf16[2,92,1,8,5,16]{5,3,4,1,0,2:T(8,128)(2,1)S(1)} %copy.47), kind=kOutput, calls=%fused_computation.13 | convolution fusion | flops 718295040 | bytes 7202840 | tf_op jit(solution)/shard_map/conv_general_dilated | solution.py:23
  34.4 9.0 %copy.48 = f32[2,90,8,3,384]{4,0,3,2,1:T(2,128)} copy(f32[2,90,8,3,384]{4,2,3,1,0:T(8,128)} %broadcast_select_fusion) | data formatting | bytes 13271040 | tf_op jit(solution)/shard_map/conv_general_dilated | solution.py:23
  43.4 0.0 copy-start.3
  43.4 3.8 %slice.11 = f32[2,90,1,16,384]{4,0,3,1,2:T(2,128)S(1)} slice(f32[2,90,1,24,384]{4,0,3,1,2:T(2,128)} %bitcast.44), slice={[0:2], [0:90], [0:1], [0:16], [0:384]} | slice | bytes 8847360 | tf_op jit(solution)/shard_map/conv_general_dilated | solution.py:23
  47.2 0.0 copy-start.1
  47.2 2.0 %copy-done.1 = f32[2,90,1,16,384]{4,0,3,1,2:T(2,128)} copy-done((f32[2,90,1,16,384]{4,0,3,1,2:T(2,128)}, f32[2,90,1,16,384]{4,0,3,1,2:T(2,128)S(1)}, u32[]{:S(2)}) %copy-start.1) | copy-done | bytes 4423704
  49.2 0.0 copy-done.3
  49.2 0.5 multiply_reduce_fusion
  49.7 0.1 copy.50
  49.8 0.1 copy.51
  49.9 0.0 copy-done.5
  49.9 3.4 %multiply_convert_fusion = bf16[2,90,16,384]{3,2,1,0:T(8,128)(2,1)S(1)} fusion(f32[2,90,1,16,384]{4,0,3,1,2:T(2,128)} %copy-done.1, f32[384]{0:T(512)S(1)} %copy-done.5, f32[2,90,16]{2,1,0:T(8,128)S(1)} %copy.51, f32[384]{0:T(512)S(1)} %copy-done.3), kind=kLoop, calls=%fused_computation.11 | loop fusion | flops 8847360 | bytes 6650112 | tf_op jit(solution)/shard_map/convert_element_type | solution.py:35
  53.3 0.2 pad_bitcast_fusion
  53.5 0.5 copy.62
  54.0 0.4 pad.17.clone
  54.4 1.3 %copy.54 = bf16[2,92,1,8,3,384]{5,3,4,1,0,2:T(8,128)(2,1)S(1)} copy(bf16[2,92,1,8,3,384]{5,1,4,3,0,2:T(8,128)(2,1)S(1)} %bitcast.45) | data formatting | bytes 6782976 | tf_op jit(solution)/shard_map/conv_general_dilated | solution.py:23
  55.7 0.6 slice.12
  56.3 0.0 copy-done
  56.3 24.6 %fusion.12 = f32[2,90,8,3,24]{4,2,3,1,0:T(8,128)S(1)} fusion(bf16[3,3,3,384,24]{3,4,2,1,0:T(8,128)(2,1)S(1)} %copy-done, bf16[2,92,1,7,2,384]{5,3,4,1,0,2:T(8,128)(2,1)S(1)} %slice.12, bf16[2,92,1,8,3,384]{5,3,4,1,0,2:T(8,128)(2,1)S(1)} %copy.54, pred[8,3]{0,1:T(4,128)(4,1)S(1)} %copy-done.4), kind=kOutput, calls=%fused_computation.19 | convolution fusion | flops 1092015360 | bytes 6282264 | tf_op jit(solution)/shard_map/conv_general_dilated | solution.py:23
  80.9 0.8 copy.55
  81.7 1.3 %copy.60 = f32[2,90,1,16,24]{4,3,0,1,2:T(8,128)S(1)} copy(f32[2,90,1,16,24]{1,4,3,2,0:T(8,128)S(1)} %slice.13) | data formatting | bytes 552960
  83.0 0.8 dynamic_slice.3
  83.8 0.2 fusion.11
  83.9 0.1 pad.14
  84.1 0.0 copy-done.6
  84.1 0.1 iota_compare_fusion.2
  84.2 0.1 copy.57
  84.3 0.1 reduce
  84.4 0.8 gather_fusion
  85.2 1.2 %fusion.22 = bf16[16,9,2,16,24]{4,3,2,1,0:T(8,128)(2,1)} fusion(bf16[16,2,9,16,24]{4,3,1,2,0:T(8,128)(2,1)S(1)} %gather_fusion, pred[16,9]{1,0:T(8,128)(4,1)S(1)} %iota_compare_fusion.2), kind=kLoop, calls=%fused_computation.34 | loop fusion | flops 110592 | bytes 442512
  86.4 2.9 %reshape.111 = bf16[16,2,3456]{2,1,0:T(2,128)(2,1)S(1)} reshape(bf16[16,9,2,16,24]{4,3,2,1,0:T(8,128)(2,1)} %fusion.22) | data formatting | bytes 442368
  89.3 13.6 %all_to_all.18 = bf16[16,2,3456]{2,1,0:T(2,128)(2,1)S(1)} all-to-all(bf16[16,2,3456]{2,1,0:T(2,128)(2,1)S(1)} %reshape.111), channel_id=1, replica_groups=mesh['req'=32,'sp'=16] {'sp'}, dimensions={0} | all-to-all | bytes 442368 | tf_op jit(solution)/shard_map/all_to_all | solution.py:64
  102.9 1.6 %reshape.112 = bf16[16,9,2,16,24]{4,3,2,1,0:T(8,128)(2,1)S(1)} reshape(bf16[16,2,3456]{2,1,0:T(2,128)(2,1)S(1)} %all_to_all.18) | data formatting | bytes 442368
  104.5 0.2 bitcast_bitcast_fusion
  104.8 0.5 copy.58
  105.2 2.0 %all_to_all.16 = bf16[1,2,9,16,384]{4,3,2,1,0:T(8,128)(2,1)} reshape(bf16[1,2,9,16,16,24]{5,4,3,2,1,0:T(8,128)(2,1)S(1)} %copy.58) | data formatting | bytes 442368 | tf_op jit(solution)/shard_map/all_to_all | solution.py:64
  (8 shorter events, 0.1 us)
Async XLA Ops:
  0.0 56.3 %copy-start = (bf16[3,3,3,384,24]{3,4,2,1,0:T(8,128)(2,1)S(1)}, bf16[3,3,3,384,24]{3,4,2,1,0:T(8,128)(2,1)}, u32[]{:S(2)}) copy-start(bf16[3,3,3,384,24]{3,4,2,1,0:T(8,128)(2,1)} %param.12) | copy-start | bytes 1492996
  25.7 2.6 %copy-start.2 = (bf16[3,3,3,16,384]{4,3,2,1,0:T(8,128)(2,1)S(1)}, bf16[3,3,3,16,384]{4,3,2,1,0:T(8,128)(2,1)}, u32[]{:S(2)}) copy-start(bf16[3,3,3,16,384]{4,3,2,1,0:T(8,128)(2,1)} %param.9) | copy-start | bytes 995332
  25.7 2.6 %copy-start.4 = (pred[8,3]{0,1:T(4,128)(4,1)S(1)}, pred[8,3]{0,1:T(4,128)(4,1)}, u32[]{:S(2)}) copy-start(pred[8,3]{0,1:T(4,128)(4,1)} %constant.47) | copy-start | bytes 76
  43.4 5.8 %copy-start.3 = (f32[384]{0:T(512)S(1)}, f32[384]{0:T(512)}, u32[]{:S(2)}) copy-start(f32[384]{0:T(512)} %param.10) | copy-start | bytes 4612
  47.2 2.0 %copy-start.1 = (f32[2,90,1,16,384]{4,0,3,1,2:T(2,128)}, f32[2,90,1,16,384]{4,0,3,1,2:T(2,128)S(1)}, u32[]{:S(2)}) copy-start(f32[2,90,1,16,384]{4,0,3,1,2:T(2,128)S(1)} %slice.11) | copy-start | bytes 13271044
  49.2 0.7 copy-start.5
  81.6 2.5 %copy-start.6 = (s32[16]{0:T(128)S(1)}, s32[16]{0:T(128)}, u32[]{:S(2)}) copy-start(s32[16]{0:T(128)} %param.8) | copy-start | bytes 196
where the time goes:
time: 107 us
  blocking collectives  39 us (36%)
  local copies, waits for them, and re-layouts  31.9 us (30%)
  matrix products  30.6 us (29%)
  other arithmetic  5.55 us (5%)
    conv_general_dilated x2, matrix products, causal_conv(): lax.conv_general_dilated(field[None], filters, (1, 1, 1), [(2, 0), (0, 0)...  30.6 us
    all_gather x1, blocking collectives, per_device(): everything = lax.all_gather(tokens, 'sp', axis=0, tiled=True)  25.4 us
    conv_general_dilated x8, local copies, waits for them, and re-layouts, causal_conv(): lax.conv_general_dilated(field[None], filters, (1, 1, 1), [(2, 0), (0, 0)...  16.7 us
    all_to_all x1, blocking collectives, per_device(): lax.all_to_all(for_sending(outgoing), 'sp', split_axis=0, concat_axis=4,...  13.6 us
    unnamed x19, local copies, waits for them, and re-layouts  9.05 us
    convert_element_type x1, other arithmetic, activate(): return jax.nn.silu(first * scale * norm_gain).astype(jnp.bfloat16)  3.35 us
    all_to_all x3, local copies, waits for them, and re-layouts, per_device(): lax.all_to_all(for_sending(outgoing), 'sp', split_axis=0, concat_axis=4,...  2.63 us

commit v1 on v0

v1 whole, which is shorter than its diff:
```python
import jax
import jax.numpy as jnp
from jax import lax
from jax.experimental import pallas as pl
from jax.experimental.pallas import tpu as pltpu
from jax.sharding import PartitionSpec as P

C = 16
FR = 2
PH = 45
PW = 8
N = 16
TOK = FR * PH * PW // N
HALF = 32
FL = 384
LIVE = PH * PW
C2 = 384
CO = 24
TILES = 13
BLK = 32
CHUNK = 256
MESH = pl.DeviceIdType.MESH
F32, BF16 = jnp.float32, jnp.bfloat16


def peer(i):
    return {"sp": i}


def step_of(t):
    up = (t + 1) // 2
    return 8 + up * (1 - 2 * ((t + 1) % 2))


def col_iota(shape):
    return lax.broadcasted_iota(jnp.int32, shape, len(shape) - 1)


def row_iota(shape):
    return lax.broadcasted_iota(jnp.int32, shape, len(shape) - 2)


def shift_of(phase, d):
    moved = phase + d
    return moved % 2, moved // 2


def prepare(f_ref, b1_ref, gain_ref, b2_ref, me, ft, ft0, ghalf, b2col, place, xp):
    tap1, tap2 = f_ref[0].astype(F32), f_ref[1].astype(F32)
    bias = b1_ref[...]
    hi = bias.astype(BF16).astype(F32)
    mid = (bias - hi).astype(BF16).astype(F32)
    low = bias - hi - mid
    rows = row_iota((16, C2))
    bias_rows = jnp.where(rows == 0, hi, jnp.where(rows == 1, mid, jnp.where(rows == 2, low, 0.0)))
    ft[...] = jnp.concatenate([tap2, bias_rows, tap1, jnp.zeros((80, C2), F32)], 0).T[:, :304].astype(BF16)
    ft0[...] = jnp.concatenate([bias_rows, tap2, jnp.zeros((96, C2), F32)], 0).T[:, :160].astype(BF16)
    ghalf[...] = jnp.broadcast_to(gain_ref[...] * 0.5, (128, C2)).T
    b2col[...] = jnp.broadcast_to(b2_ref[...], (128, C2)).T
    shape = (256, FL)
    token = row_iota(shape)
    src, i = token // HALF, token % HALF
    lane = col_iota(shape)
    one, zero = jnp.ones(shape, F32), jnp.zeros(shape, F32)
    place[0] = jnp.where(lane == src * TOK + i, one, zero).astype(BF16)
    place[1] = jnp.where((lane == src * TOK + HALF + i) & (i < TOK - HALF), one, zero).astype(BF16)
    xp[144:160, :] = jnp.ones((16, 4 * FL), BF16)


def patches(tok_all, place, xp):
    halves = [tok_all[8 * f:8 * f + 8].reshape(256, 128).astype(F32).T.astype(BF16) for f in range(FR)]
    left = jnp.concatenate([h[:64] for h in halves], 0)
    right = jnp.concatenate([h[64:] for h in halves], 0)
    grid = jnp.dot(left, place[0], preferred_element_type=F32) + jnp.dot(right, place[1], preferred_element_type=F32)
    q = col_iota((1, FL)) % PW
    for f in range(FR):
        for a2 in range(2):
            for b2 in range(2):
                at = f * 64 + (a2 * 2 + b2) * C
                field = grid[at:at + C]
                moved = {}
                for sr in ((0, -1) if a2 == 1 else (0, 1)):
                    for sq in ((0, -1) if b2 == 1 else (0, 1)):
                        piece = field
                        if sr or sq:
                            piece = pltpu.roll(piece, (-(PW * sr + sq)) % FL, 1)
                        if sq:
                            piece = jnp.where(q == (0 if sq < 0 else PW - 1), 0.0, piece)
                        moved[sr, sq] = piece.astype(BF16)
                for a in range(2):
                    for b in range(2):
                        for dy in range(3):
                            for dx in range(3):
                                sa, sr = shift_of(a, dy - 1)
                                sb, sq = shift_of(b, dx - 1)
                                if (sa, sb) == (a2, b2):
                                    row = (160 if f == 0 else 0) + (dy * 3 + dx) * C
                                    ph = a * 2 + b
                                    xp[row:row + C, ph * FL:(ph + 1) * FL] = moved[sr, sq]


def convolve(f, xp, ft, ft0, ghalf, wcat, hid, prod):
    for at in range(0, 4 * FL, CHUNK):
        lanes = slice(at, at + CHUNK)
        if f == 0:
            first = jnp.dot(ft0[...], xp[144:304, lanes], preferred_element_type=F32)
        else:
            first = jnp.dot(ft[...], xp[:, lanes], preferred_element_type=F32)
        mean = jnp.sum(first * first, axis=0, keepdims=True) * (1.0 / C2)
        live = (col_iota((1, CHUNK)) + at) % FL < LIVE
        scale = jnp.where(live, lax.rsqrt(mean + 1e-6), 0.0)
        gain = jnp.concatenate([ghalf[...]] * (CHUNK // 128), 1)
        u = first * scale * gain
        h = (u + u * jnp.tanh(u)).astype(BF16)
        hid[f * C2:(f + 1) * C2, lanes] = h
        if f == 0:
            prod[:, lanes] = jnp.dot(wcat[:, C2:], h, preferred_element_type=F32)
        else:
            prod[:, lanes] = jnp.dot(wcat[...], hid[:, lanes], preferred_element_type=F32)


def gather_taps(f, me, prod, b2col, fin):
    q = col_iota((1, FL)) % PW
    bias = b2col[pl.ds(pl.multiple_of(me * CO, 8), CO), :]
    bias = jnp.concatenate([bias] * (FL // 128), 1)
    outs = []
    for a in range(2):
        for b in range(2):
            sums = {}
            for dy in range(3):
                for dx in range(3):
                    sa, sr = shift_of(a, dy - 1)
                    sb, sq = shift_of(b, dx - 1)
                    tap, ph = dy * 3 + dx, sa * 2 + sb
                    term = prod[tap * CO:(tap + 1) * CO, ph * FL:(ph + 1) * FL]
                    sums[sr, sq] = sums[sr, sq] + term if (sr, sq) in sums else term
            sr, sq = (-1, 1)[a], (-1, 1)[b]
            side = sums[0, sq] + pltpu.roll(sums[sr, sq], (-PW * sr) % FL, 1)
            side = pltpu.roll(side, (-sq) % FL, 1)
            side = jnp.where(q == (0 if sq < 0 else PW - 1), 0.0, side)
            outs.append(sums[0, 0] + pltpu.roll(sums[sr, 0], (-PW * sr) % FL, 1) + side + bias)
    block = col_iota((1, 128)) // 32
    for t in range(FL // 128):
        for j in range(4):
            tile = None
            for ph in range(4):
                piece = outs[ph][:, 128 * t:128 * t + 128]
                if ph != j:
                    piece = pltpu.roll(piece, (32 * (ph - j)) % 128, 1)
                tile = piece if tile is None else jnp.where(block == ph, piece, tile)
            fin[f, 4 * t + j] = tile
    fin[f, TILES - 1] = jnp.zeros((CO, 128), F32)


def strip_block(f, start, fin):
    r0 = start // 2
    tile, off = r0 // 4, r0 % 4
    one, two = fin[f, tile], fin[f, tile + 1]
    row = (col_iota((1, 128)) % 32) // PW
    two = pltpu.roll(two, (32 - PW * off) % 128, 1)
    main = jnp.where(row + off < 4, pltpu.roll(one, (128 - PW * off) % 128, 1), two)
    fifth = pltpu.roll(two, 96, 1)
    packed = jnp.where(row == 0, fifth[:8], jnp.where(row == 1, pltpu.roll(fifth[8:16], PW, 1), pltpu.roll(fifth[16:], 2 * PW, 1)))
    return jnp.concatenate([main, packed], 0).astype(BF16)


def main_kernel(
    rows_ref, tok_ref, f_ref, b1_ref, gain_ref, w_ref, b2_ref, recv,
    tokv, fv, b1v, gainv, b2v, pack, tok_all, ft, ft0, ghalf, b2col, place, wcat, xp, hid, prod, fin, send, starts,
    local_sem, tok_send, tok_recv, out_send, out_recv,
):
    me = lax.axis_index("sp")
    barrier = pltpu.get_barrier_semaphore()

    def greet(i, carry):
        pl.semaphore_signal(barrier, inc=1, device_id=peer(lax.rem(me + i, N)), device_id_type=MESH)
        return carry

    lax.fori_loop(1, N, greet, 0)

    copies = [
        (tok_ref, tokv), (f_ref.at[1], fv.at[0]), (f_ref.at[2], fv.at[1]), (b1_ref, b1v), (gain_ref, gainv), (b2_ref, b2v),
        (w_ref.at[1], wcat.at[:, 0:C2]), (w_ref.at[2], wcat.at[:, C2:2 * C2]),
    ]
    copies = [pltpu.make_async_copy(s, d, local_sem.at[i]) for i, (s, d) in enumerate(copies)]
    for copy in copies:
        copy.start()

    def begin(i, start):
        starts[i] = start
        return start + rows_ref[i]

    lax.fori_loop(0, N, begin, 0)

    copies[0].wait()
    tokens = tokv[...].astype(F32)
    right = jnp.concatenate([tokens[HALF:], jnp.zeros((2 * HALF - TOK, 64), F32)], 0)
    block = jnp.concatenate([tokens[:HALF], right], 1).astype(BF16)
    pack[...] = block
    tok_all[me] = block
    pl.semaphore_wait(barrier, N - 1)

    def tok_copy(to, src):
        return pltpu.make_async_remote_copy(
            src_ref=pack, dst_ref=tok_all.at[src], send_sem=tok_send.at[to], recv_sem=tok_recv.at[src],
            device_id=peer(to), device_id_type=MESH,
        )

    def tok_start(t, carry):
        tok_copy(lax.rem(me + step_of(t), N), me).start()
        return carry

    lax.fori_loop(0, N - 1, tok_start, 0)

    for copy in copies[1:]:
        copy.wait()
    prepare(fv, b1v, gainv, b2v, me, ft, ft0, ghalf, b2col, place, xp)

    def tok_wait(i, carry):
        src = lax.rem(me + i, N)
        tok_copy(src, src).wait_recv()
        return carry

    lax.fori_loop(1, N, tok_wait, 0)
    patches(tok_all, place, xp)

    def out_copy(f, to, src):
        return pltpu.make_async_remote_copy(
            src_ref=send.at[f, to], dst_ref=recv.at[src, f], send_sem=out_send.at[f, to], recv_sem=out_recv.at[f, src],
            device_id=peer(to), device_id_type=MESH,
        )

    for f in range(FR):
        convolve(f, xp, ft, ft0, ghalf, wcat, hid, prod)
        gather_taps(f, me, prod, b2col, fin)

        def out_start(t, carry):
            to = lax.rem(me + step_of(t), N)
            send[f, to] = strip_block(f, starts[to], fin)
            out_copy(f, to, me).start()
            return carry

        lax.fori_loop(0, N - 1, out_start, 0)
        recv[me, f] = strip_block(f, starts[me], fin)

    def out_wait(i, carry):
        other = lax.rem(me + i, N)
        for f in range(FR):
            out_copy(f, other, other).wait()
        tok_copy(other, other).wait_send()
        return carry

    lax.fori_loop(1, N, out_wait, 0)


def exchange(strip_rows, tokens, f, b1, gain, w, b2):
    anywhere = pl.BlockSpec(memory_space=pl.ANY)
    return pl.pallas_call(
        main_kernel,
        out_shape=pltpu.VMEM((N, FR, BLK, 128), BF16),
        in_specs=[pl.BlockSpec(memory_space=pltpu.SMEM)] + [anywhere] * 6,
        out_specs=pl.BlockSpec(memory_space=pltpu.VMEM),
        scratch_shapes=[
            pltpu.VMEM((TOK, 64), BF16),
            pltpu.VMEM((2, 144, C2), BF16),
            pltpu.VMEM((1, C2), F32),
            pltpu.VMEM((1, C2), F32),
            pltpu.VMEM((1, C2), F32),
            pltpu.VMEM((HALF, 128), BF16),
            pltpu.VMEM((N, HALF, 128), BF16),
            pltpu.VMEM((C2, 304), BF16),
            pltpu.VMEM((C2, 160), BF16),
            pltpu.VMEM((C2, 128), F32),
            pltpu.VMEM((C2, 128), F32),
            pltpu.VMEM((2, 256, FL), BF16),
            pltpu.VMEM((9 * CO, 2 * C2), BF16),
            pltpu.VMEM((304, 4 * FL), BF16),
            pltpu.VMEM((2 * C2, 4 * FL), BF16),
            pltpu.VMEM((9 * CO, 4 * FL), F32),
            pltpu.VMEM((FR, TILES, CO, 128), F32),
            pltpu.VMEM((FR, N, BLK, 128), BF16),
            pltpu.SMEM((N,), jnp.int32),
            pltpu.SemaphoreType.DMA((8,)),
            pltpu.SemaphoreType.DMA((N,)),
            pltpu.SemaphoreType.DMA((N,)),
            pltpu.SemaphoreType.DMA((FR, N)),
            pltpu.SemaphoreType.DMA((FR, N)),
        ],
        compiler_params=pltpu.CompilerParams(collective_id=0, has_side_effects=True, vmem_limit_bytes=40 << 20),
    )(strip_rows, tokens, f, b1, gain, w, b2)


def assemble_kernel(rows_ref, recv, out):
    me = lax.axis_index("sp")

    def begin(i, start):
        return start + jnp.where(i < me, rows_ref[i], 0)

    start = lax.fori_loop(0, N, begin, 0)
    count = rows_ref[me]
    shape = (9 * 16, 256)
    p, lane = row_iota(shape), col_iota(shape)
    k, col = p // 16, p % 16
    odd = start % 2
    row = odd + k
    phase = (row % 2) * 2 + col % 2
    patch_row = row // 2
    at = phase * 32 + col // 2 + jnp.where(patch_row < 4, patch_row * PW, 128)
    pick = jnp.where((lane == at) & (k < count), 1.0, 0.0).astype(BF16)
    for f in range(FR):
        block = recv[:, f].astype(F32)
        main = block[:, :CO].reshape(C2, 128)
        tail = block[:, CO:]
        tail = jnp.concatenate([tail, pltpu.roll(tail, 128 - PW, 2), pltpu.roll(tail, 128 - 2 * PW, 2)], 1).reshape(C2, 128)
        both = jnp.concatenate([main, tail], 1).astype(BF16)
        strip = lax.dot_general(pick, both, (((1,), (1,)), ((), ())), preferred_element_type=F32)
        out[0, f] = strip.astype(BF16).reshape(9, 16, C2)


def assemble(strip_rows, recv):
    return pl.pallas_call(
        assemble_kernel,
        out_shape=jax.ShapeDtypeStruct((1, FR, 9, 16, C2), BF16),
        in_specs=[pl.BlockSpec(memory_space=pltpu.SMEM), pl.BlockSpec(memory_space=pltpu.VMEM)],
        out_specs=pl.BlockSpec(memory_space=pltpu.VMEM),
        compiler_params=pltpu.CompilerParams(vmem_limit_bytes=20 << 20),
    )(strip_rows, recv)


def per_device(tokens, strip_rows, first_filter, first_bias, norm_gain, second_filter, second_bias):
    f = first_filter.reshape(3, 9 * C, C2)
    w = jnp.transpose(second_filter, (0, 1, 2, 4, 3)).reshape(3, 9 * CO, C2)
    row = lambda v: v.reshape(1, C2)
    recv = exchange(strip_rows, tokens, f, row(first_bias), row(norm_gain), w, row(second_bias))
    return assemble(strip_rows, recv)


def solution(mesh):
    in_specs = (P(("req", "sp"), None), P(), P(), P(), P(), P(None, None, None, None, "sp"), P())
    out_specs = P(("req", "sp"), None, None, None, None)
    return jax.shard_map(
        per_device, mesh=mesh, in_specs=in_specs, out_specs=out_specs, check_vma=False
    )
```

time: 107 us -> 38.8 us (0.36)
  blocking collectives: 39 us -> 0 us
  Pallas kernels: 0 us -> 34.4 us
  matrix products: 30.6 us -> 0 us
  local copies, waits for them, and re-layouts: 31.9 us -> 4.09 us
  other arithmetic: 5.55 us -> 0 us
    pallas_call x0 -> x2, Pallas kernels: none -> 34.4 us  [the longest x1 32.7 us: exchange(): pl.pallas_call(main_kernel, out_shape=pltpu.VMEM((N, FR, BLK, 128), BF16)...]
    conv_general_dilated x2 -> x0, matrix products: 30.6 us -> none  [causal_conv(): lax.conv_general_dilated(field[None], filters, (1, 1, 1), [(2, 0), (0, 0)...]
    all_gather x1 -> x0, blocking collectives: 25.4 us -> none  [per_device(): everything = lax.all_gather(tokens, 'sp', axis=0, tiled=True)]
    conv_general_dilated x8 -> x0, local copies, waits for them, and re-layouts: 16.7 us -> none  [causal_conv(): lax.conv_general_dilated(field[None], filters, (1, 1, 1), [(2, 0), (0, 0)...]
    all_to_all x1 -> x0, blocking collectives: 13.6 us -> none  [per_device(): lax.all_to_all(for_sending(outgoing), 'sp', split_axis=0, concat_axis=4,...]
    unnamed x19 -> x8, local copies, waits for them, and re-layouts: 9.05 us -> 2.01 us
    convert_element_type x2 -> x0, other arithmetic: 3.51 us -> none  [the longest x1 3.35 us: activate(): return jax.nn.silu(first * scale * norm_gain).astype(jnp.bfloat16)]
    all_to_all x3 -> x0, local copies, waits for them, and re-layouts: 2.63 us -> none  [per_device(): lax.all_to_all(for_sending(outgoing), 'sp', split_axis=0, concat_axis=4,...]
where the time goes in v1:
time: 38.8 us; the launch traced here: 38.5 us
  Pallas kernels  34.4 us (89%)
  local copies, waits for them, and re-layouts  4.09 us (11%)
    pallas_call x1, Pallas kernels, exchange(): pl.pallas_call(main_kernel, out_shape=pltpu.VMEM((N, FR, BLK, 128), BF16)...  32.7 us
    reshape x3, local copies, waits for them, and re-layouts, per_device(): row = lambda v: v.reshape(1, C2)  2.08 us
    unnamed x8, local copies, waits for them, and re-layouts  2.01 us
    pallas_call x1, Pallas kernels, assemble(): pl.pallas_call(assemble_kernel, out_shape=jax.ShapeDtypeStruct((1, FR, 9,...  1.67 us

profile of v1, /device:TPU:1, one launch (start us, length us, event | category | flops | bytes accessed | tf_op | source)
XLA Modules:
  0.0 38.5 jit_solution(5461479266194525864)
XLA Ops:
  0.0 0.0 copy-start.2
  0.0 0.7 %reshape.16.b1_ref = f32[1,384]{1,0:T(1,128)S(1)} reshape(f32[384]{0:T(512)} %param.10) | data formatting | bytes 3072 | tf_op jit(solution)/shard_map/reshape | solution.py:333
  0.7 0.7 %reshape.17.gain_ref = f32[1,384]{1,0:T(1,128)S(1)} reshape(f32[384]{0:T(512)} %param.11) | data formatting | bytes 3072 | tf_op jit(solution)/shard_map/reshape | solution.py:333
  1.4 0.0 copy-start.3
  1.4 0.7 %reshape.19.b2_ref = f32[1,384]{1,0:T(1,128)S(1)} reshape(f32[384]{0:T(512)} %param.13) | data formatting | bytes 3072 | tf_op jit(solution)/shard_map/reshape | solution.py:333
  2.1 0.0 copy-done.2
  2.1 0.0 copy-done.3
  2.1 0.0 copy-start
  2.1 1.0 %copy-done = bf16[3,3,3,384,24]{3,4,2,1,0:T(8,128)(2,1)S(1)} copy-done((bf16[3,3,3,384,24]{3,4,2,1,0:T(8,128)(2,1)S(1)}, bf16[3,3,3,384,24]{3,4,2,1,0:T(8,128)(2,1)}, u32[]{:S(2)}) %copy-start) | copy-done | bytes 497688
  3.1 0.0 copy-start.1
  3.1 1.0 %copy-done.1 = bf16[3,3,3,16,384]{4,3,2,1,0:T(8,128)(2,1)S(1)} copy-done((bf16[3,3,3,16,384]{4,3,2,1,0:T(8,128)(2,1)S(1)}, bf16[3,3,3,16,384]{4,3,2,1,0:T(8,128)(2,1)}, u32[]{:S(2)}) %copy-start.1) | copy-done | bytes 331800
  4.1 32.7 %shard_map.73.recv = bf16[16,2,32,128]{3,2,1,0:T(8,128)(2,1)S(1)} custom-call(s32[16]{0:T(128)S(1)} %copy-done.3, bf16[45,64]{1,0:T(8,128)(2,1)S(1)} %copy-done.2, bf16[3,144,384]{2,1,0:T(8,128)(2,1)S(1)} %bitcast.5, f32[1,384]{1,0:T(1,128)S(1)} %reshape.16.b1_ref, f32[1,384]{1,0:T(1,128)S(1)} %reshape.17.gain_ref, bf16[3,216,384]{2,1,0:T(8,128)(2,1)S(1)} %bitcast.4, ...), custom_call_target="tpu_custom_call" | custom-call | tf_op jit(solution)/shard_map/pallas_call | solution.py:258
  36.8 1.7 %shard_map.74 = bf16[1,2,9,16,384]{4,3,2,1,0:T(8,128)(2,1)} custom-call(s32[16]{0:T(128)S(1)} %copy-done.3, bf16[16,2,32,128]{3,2,1,0:T(8,128)(2,1)S(1)} %shard_map.73.recv), custom_call_target="tpu_custom_call" | custom-call | tf_op jit(solution)/shard_map/pallas_call | solution.py:321
Async XLA Ops:
  0.0 2.1 %copy-start.2 = (bf16[45,64]{1,0:T(8,128)(2,1)S(1)}, bf16[45,64]{1,0:T(8,128)(2,1)}, u32[]{:S(2)}) copy-start(bf16[45,64]{1,0:T(8,128)(2,1)} %tok_ref.1) | copy-start | bytes 17284
  1.4 0.7 %copy-start.3 = (s32[16]{0:T(128)S(1)}, s32[16]{0:T(128)}, u32[]{:S(2)}) copy-start(s32[16]{0:T(128)} %rows_ref.3) | copy-start | bytes 196
  2.1 1.0 %copy-start = (bf16[3,3,3,384,24]{3,4,2,1,0:T(8,128)(2,1)S(1)}, bf16[3,3,3,384,24]{3,4,2,1,0:T(8,128)(2,1)}, u32[]{:S(2)}) copy-start(bf16[3,3,3,384,24]{3,4,2,1,0:T(8,128)(2,1)} %param.12) | copy-start | bytes 1492996
  3.1 1.0 %copy-start.1 = (bf16[3,3,3,16,384]{4,3,2,1,0:T(8,128)(2,1)S(1)}, bf16[3,3,3,16,384]{4,3,2,1,0:T(8,128)(2,1)}, u32[]{:S(2)}) copy-start(bf16[3,3,3,16,384]{4,3,2,1,0:T(8,128)(2,1)} %param.9) | copy-start | bytes 995332

commit v2 on v1

--- a/solution.py
+++ b/solution.py
@@ -166,7 +166,7 @@
 
 def main_kernel(
     rows_ref, tok_ref, f_ref, b1_ref, gain_ref, w_ref, b2_ref, recv,
-    tokv, fv, b1v, gainv, b2v, pack, tok_all, ft, ft0, ghalf, b2col, place, wcat, xp, hid, prod, fin, send, starts,
+    rows, tokv, fv, b1v, gainv, b2v, pack, tok_all, ft, ft0, ghalf, b2col, place, wcat, xp, hid, prod, fin, send, starts,
     local_sem, tok_send, tok_recv, out_send, out_recv,
 ):
     me = lax.axis_index("sp")
@@ -179,18 +179,12 @@
     lax.fori_loop(1, N, greet, 0)
 
     copies = [
-        (tok_ref, tokv), (f_ref.at[1], fv.at[0]), (f_ref.at[2], fv.at[1]), (b1_ref, b1v), (gain_ref, gainv), (b2_ref, b2v),
-        (w_ref.at[1], wcat.at[:, 0:C2]), (w_ref.at[2], wcat.at[:, C2:2 * C2]),
+        (tok_ref, tokv), (f_ref.at[1], fv.at[0]), (f_ref.at[2], fv.at[1]), (b1_ref, b1v.at[0]), (gain_ref, gainv.at[0]), (b2_ref, b2v.at[0]),
+        (w_ref.at[1], wcat.at[:, 0:C2]), (w_ref.at[2], wcat.at[:, C2:2 * C2]), (rows_ref, rows),
     ]
     copies = [pltpu.make_async_copy(s, d, local_sem.at[i]) for i, (s, d) in enumerate(copies)]
     for copy in copies:
         copy.start()
-
-    def begin(i, start):
-        starts[i] = start
-        return start + rows_ref[i]
-
-    lax.fori_loop(0, N, begin, 0)
 
     copies[0].wait()
     tokens = tokv[...].astype(F32)
@@ -214,6 +208,12 @@
 
     for copy in copies[1:]:
         copy.wait()
+
+    def begin(i, start):
+        starts[i] = start
+        return start + rows[i]
+
+    lax.fori_loop(0, N, begin, 0)
     prepare(fv, b1v, gainv, b2v, me, ft, ft0, ghalf, b2col, place, xp)
 
     def tok_wait(i, carry):
@@ -254,13 +254,14 @@
 
 
 def exchange(strip_rows, tokens, f, b1, gain, w, b2):
-    anywhere = pl.BlockSpec(memory_space=pl.ANY)
+    hbm = pl.BlockSpec(memory_space=pltpu.HBM)
     return pl.pallas_call(
         main_kernel,
         out_shape=pltpu.VMEM((N, FR, BLK, 128), BF16),
-        in_specs=[pl.BlockSpec(memory_space=pltpu.SMEM)] + [anywhere] * 6,
+        in_specs=[hbm] * 7,
         out_specs=pl.BlockSpec(memory_space=pltpu.VMEM),
         scratch_shapes=[
+            pltpu.SMEM((N,), jnp.int32),
             pltpu.VMEM((TOK, 64), BF16),
             pltpu.VMEM((2, 144, C2), BF16),
             pltpu.VMEM((1, C2), F32),
@@ -280,14 +281,14 @@
             pltpu.VMEM((FR, TILES, CO, 128), F32),
             pltpu.VMEM((FR, N, BLK, 128), BF16),
             pltpu.SMEM((N,), jnp.int32),
-            pltpu.SemaphoreType.DMA((8,)),
+            pltpu.SemaphoreType.DMA((9,)),
             pltpu.SemaphoreType.DMA((N,)),
             pltpu.SemaphoreType.DMA((N,)),
             pltpu.SemaphoreType.DMA((FR, N)),
             pltpu.SemaphoreType.DMA((FR, N)),
         ],
         compiler_params=pltpu.CompilerParams(collective_id=0, has_side_effects=True, vmem_limit_bytes=40 << 20),
-    )(strip_rows, tokens, f, b1, gain, w, b2)
+    )(*(pltpu.with_memory_space_constraint(v, pltpu.HBM) for v in (strip_rows, tokens, f, b1, gain, w, b2)))
 
 
 def assemble_kernel(rows_ref, recv, out):
@@ -330,8 +331,7 @@
 def per_device(tokens, strip_rows, first_filter, first_bias, norm_gain, second_filter, second_bias):
     f = first_filter.reshape(3, 9 * C, C2)
     w = jnp.transpose(second_filter, (0, 1, 2, 4, 3)).reshape(3, 9 * CO, C2)
-    row = lambda v: v.reshape(1, C2)
-    recv = exchange(strip_rows, tokens, f, row(first_bias), row(norm_gain), w, row(second_bias))
+    recv = exchange(strip_rows, tokens, f, first_bias, norm_gain, w, second_bias)
     return assemble(strip_rows, recv)
 
 

time: 38.8 us -> 34.3 us (0.88)
  local copies, waits for them, and re-layouts: 4.09 us -> 0.01 us
    reshape x3 -> x0, local copies, waits for them, and re-layouts: 2.08 us -> none  [per_device(): row = lambda v: v.reshape(1, C2)]
    unnamed x8 -> x2, local copies, waits for them, and re-layouts: 2.01 us -> 0.01 us
where the time goes in v2:
time: 34.3 us; the launch traced here: 34.1 us
  Pallas kernels  34.1 us (99%)
    pallas_call x1, Pallas kernels, exchange(): pl.pallas_call(main_kernel, out_shape=pltpu.VMEM((N, FR, BLK, 128), BF16)...  32.5 us
    pallas_call x1, Pallas kernels, assemble(): pl.pallas_call(assemble_kernel, out_shape=jax.ShapeDtypeStruct((1, FR, 9,...  1.67 us

profile of v2, /device:TPU:1, one launch (start us, length us, event | category | flops | bytes accessed | tf_op | source)
XLA Modules:
  0.0 34.1 jit_solution(5409893453354193264)
XLA Ops:
  0.0 0.0 copy-start
  0.0 32.5 %shard_map.73.recv = bf16[16,2,32,128]{3,2,1,0:T(8,128)(2,1)S(1)} custom-call(s32[16]{0:T(128)} %rows_ref.3, bf16[45,64]{1,0:T(8,128)(2,1)} %tok_ref.1, bf16[3,144,384]{2,1,0:T(8,128)(2,1)} %bitcast.5, f32[384]{0:T(512)} %b1_ref.1, f32[384]{0:T(512)} %gain_ref.1, bf16[3,216,384]{2,1,0:T(8,128)(2,1)} %bitcast.4, f32[384]{0:T(512)} %b2_ref.1), custom_call_target="tpu_custom_call" | custom-call | tf_op jit(solution)/shard_map/pallas_call | solution.py:258
  32.5 0.0 copy-done
  32.5 1.7 %shard_map.74 = bf16[1,2,9,16,384]{4,3,2,1,0:T(8,128)(2,1)} custom-call(s32[16]{0:T(128)S(1)} %copy-done, bf16[16,2,32,128]{3,2,1,0:T(8,128)(2,1)S(1)} %shard_map.73.recv), custom_call_target="tpu_custom_call" | custom-call | tf_op jit(solution)/shard_map/pallas_call | solution.py:322
Async XLA Ops:
  0.0 32.5 %copy-start = (s32[16]{0:T(128)S(1)}, s32[16]{0:T(128)}, u32[]{:S(2)}) copy-start(s32[16]{0:T(128)} %rows_ref.3) | copy-start | bytes 196

commit v3 on v2

v3 whole, which is shorter than its diff:
```python
import jax
import jax.numpy as jnp
from jax import lax
from jax.experimental import pallas as pl
from jax.experimental.pallas import tpu as pltpu
from jax.sharding import PartitionSpec as P

C = 16
FR = 2
PH = 45
PW = 8
N = 16
TOK = FR * PH * PW // N
HALF = 24
FL = 384
LIVE = PH * PW
C2 = 384
CO = 24
TILES = 13
CHUNK = 256
MESH = pl.DeviceIdType.MESH
F32, BF16 = jnp.float32, jnp.bfloat16


def peer(i):
    return {"sp": i}


def step_of(t):
    up = (t + 1) // 2
    return 8 + up * (1 - 2 * ((t + 1) % 2))


def col_iota(shape):
    return lax.broadcasted_iota(jnp.int32, shape, len(shape) - 1)


def row_iota(shape):
    return lax.broadcasted_iota(jnp.int32, shape, len(shape) - 2)


def shift_of(phase, d):
    moved = phase + d
    return moved % 2, moved // 2


def prepare(f_ref, b1_ref, gain_ref, b2_ref, me, ft, ft0, ghalf, b2col, place, xp):
    tap1, tap2 = f_ref[0].astype(F32), f_ref[1].astype(F32)
    bias = b1_ref[...]
    hi = bias.astype(BF16).astype(F32)
    mid = (bias - hi).astype(BF16).astype(F32)
    low = bias - hi - mid
    rows = row_iota((16, C2))
    bias_rows = jnp.where(rows == 0, hi, jnp.where(rows == 1, mid, jnp.where(rows == 2, low, 0.0)))
    ft[...] = jnp.concatenate([tap2, bias_rows, tap1, jnp.zeros((80, C2), F32)], 0).T[:, :304].astype(BF16)
    ft0[...] = jnp.concatenate([bias_rows, tap2, jnp.zeros((96, C2), F32)], 0).T[:, :160].astype(BF16)
    ghalf[...] = jnp.broadcast_to(gain_ref[...] * 0.5, (128, C2)).T
    b2col[...] = jnp.broadcast_to(b2_ref[...], (128, C2)).T
    shape = (8 * HALF, FL)
    token = row_iota(shape)
    src, i = token // HALF, token % HALF
    lane = col_iota(shape)
    one, zero = jnp.ones(shape, F32), jnp.zeros(shape, F32)
    place[0] = jnp.where(lane == src * TOK + i, one, zero).astype(BF16)
    place[1] = jnp.where((lane == src * TOK + HALF + i) & (i < TOK - HALF), one, zero).astype(BF16)
    xp[144:160, :] = jnp.ones((16, 4 * FL), BF16)


def patches(f, tok_all, place, xp):
    blocks = tok_all[8 * f:8 * f + 8].astype(F32).reshape(8 * HALF, 128).T.astype(BF16)
    grid = jnp.dot(blocks[:64], place[0], preferred_element_type=F32) + jnp.dot(blocks[64:], place[1], preferred_element_type=F32)
    q = col_iota((1, FL)) % PW
    for a2 in range(2):
        for b2 in range(2):
            at = (a2 * 2 + b2) * C
            field = grid[at:at + C]
            moved = {}
            for sr in ((0, -1) if a2 == 1 else (0, 1)):
                for sq in ((0, -1) if b2 == 1 else (0, 1)):
                    piece = field
                    if sr or sq:
                        piece = pltpu.roll(piece, (-(PW * sr + sq)) % FL, 1)
                    if sq:
                        piece = jnp.where(q == (0 if sq < 0 else PW - 1), 0.0, piece)
                    moved[sr, sq] = piece.astype(BF16)
            for a in range(2):
                for b in range(2):
                    for dy in range(3):
                        for dx in range(3):
                            sa, sr = shift_of(a, dy - 1)
                            sb, sq = shift_of(b, dx - 1)
                            if (sa, sb) == (a2, b2):
                                row = (160 if f == 0 else 0) + (dy * 3 + dx) * C
                                ph = a * 2 + b
                                xp[row:row + C, ph * FL:(ph + 1) * FL] = moved[sr, sq]


def convolve(f, xp, ft, ft0, ghalf, wcat, hid, prod):
    def first_of(at):
        lanes = slice(at, at + CHUNK)
        if f == 0:
            return jnp.dot(ft0[...], xp[144:304, lanes], preferred_element_type=F32)
        return jnp.dot(ft[...], xp[:, lanes], preferred_element_type=F32)

    def second_of(at):
        lanes = slice(at, at + CHUNK)
        if f == 0:
            prod[:, lanes] = jnp.dot(wcat[:, C2:], hid[0:C2, lanes], preferred_element_type=F32)
        else:
            prod[:, lanes] = jnp.dot(wcat[...], hid[:, lanes], preferred_element_type=F32)

    def act(at, first):
        lanes = slice(at, at + CHUNK)
        mean = jnp.sum(first * first, axis=0, keepdims=True) * (1.0 / C2)
        live = (col_iota((1, CHUNK)) + at) % FL < LIVE
        scale = jnp.where(live, lax.rsqrt(mean + 1e-6), 0.0)
        gain = jnp.concatenate([ghalf[...]] * (CHUNK // 128), 1)
        u = first * scale * gain
        hid[f * C2:(f + 1) * C2, lanes] = (u + u * jnp.tanh(u)).astype(BF16)

    ats = list(range(0, 4 * FL, CHUNK))
    ready = first_of(ats[0])
    for n, at in enumerate(ats):
        ahead = first_of(ats[n + 1]) if n + 1 < len(ats) else None
        act(at, ready)
        if n:
            second_of(ats[n - 1])
        ready = ahead
    second_of(ats[-1])


def gather_taps(f, me, prod, b2col, fin, rot):
    q = col_iota((1, FL)) % PW
    bias = b2col[pl.ds(pl.multiple_of(me * CO, 8), CO), :]
    bias = jnp.concatenate([bias] * (FL // 128), 1)
    outs = []
    for a in range(2):
        for b in range(2):
            sums = {}
            for dy in range(3):
                for dx in range(3):
                    sa, sr = shift_of(a, dy - 1)
                    sb, sq = shift_of(b, dx - 1)
                    tap, ph = dy * 3 + dx, sa * 2 + sb
                    term = prod[tap * CO:(tap + 1) * CO, ph * FL:(ph + 1) * FL]
                    sums[sr, sq] = sums[sr, sq] + term if (sr, sq) in sums else term
            sr, sq = (-1, 1)[a], (-1, 1)[b]
            side = sums[0, sq] + pltpu.roll(sums[sr, sq], (-PW * sr) % FL, 1)
            side = pltpu.roll(side, (-sq) % FL, 1)
            side = jnp.where(q == (0 if sq < 0 else PW - 1), 0.0, side)
            outs.append(sums[0, 0] + pltpu.roll(sums[sr, 0], (-PW * sr) % FL, 1) + side + bias)
    block = col_iota((1, 128)) // 32
    for t in range(FL // 128):
        for j in range(4):
            tile = None
            for ph in range(4):
                piece = outs[ph][:, 128 * t:128 * t + 128]
                if ph != j:
                    piece = pltpu.roll(piece, (32 * (ph - j)) % 128, 1)
                tile = piece if tile is None else jnp.where(block == ph, piece, tile)
            fin[f, 4 * t + j] = tile
            parts = [tile[8 * m:8 * m + 8] for m in range(3)]
            parts = [pltpu.roll(v, 8 * m + 64 * f, 1) if m or f else v for m, v in enumerate(parts)]
            rot[f, 4 * t + j] = jnp.concatenate(parts, 0)
    fin[f, TILES - 1] = jnp.zeros((CO, 128), F32)
    rot[f, TILES - 1] = jnp.zeros((CO, 128), F32)


def cut_strips(f, starts, fin, rot, send):
    lane = col_iota((1, 128))
    row = (lane % 32) // PW * 2 + lane // 64
    for to in range(N):
        start = starts[to]
        tile, off = start // 8, start % 8
        main = jnp.where(row >= off, fin[f, tile], fin[f, tile + 1])
        if f == 0:
            send[to] = main.astype(BF16)
            continue
        slot = (lane // 8 + 16 - (off % 2 * 8 + off // 2)) % 16
        tail = None
        for g in range(FR):
            ninth = rot[g, tile + 1]
            for m in range(3):
                part = ninth[8 * m:8 * m + 8]
                tail = part if tail is None else jnp.where((slot // 8 == g) & (slot % 4 == m), part, tail)
        send[to] = jnp.concatenate([main, tail], 0).astype(BF16)


def main_kernel(
    rows_ref, tok_ref, f_ref, b1_ref, gain_ref, w_ref, b2_ref, recv0, recv1,
    rows, tokv, fv, b1v, gainv, b2v, pack, tok_all, ft, ft0, ghalf, b2col, place, wcat, xp, hid, prod, fin, rot, send0, send1,
    starts, local_sem, tok_send, tok_recv, out_send, out_recv,
):
    me = lax.axis_index("sp")
    barrier = pltpu.get_barrier_semaphore()

    def greet(i, carry):
        pl.semaphore_signal(barrier, inc=1, device_id=peer(lax.rem(me + i, N)), device_id_type=MESH)
        return carry

    lax.fori_loop(1, N, greet, 0)

    copies = [
        (tok_ref, tokv), (f_ref.at[1], fv.at[0]), (f_ref.at[2], fv.at[1]), (b1_ref, b1v.at[0]), (gain_ref, gainv.at[0]), (b2_ref, b2v.at[0]),
        (w_ref.at[1], wcat.at[:, 0:C2]), (w_ref.at[2], wcat.at[:, C2:2 * C2]), (rows_ref, rows),
    ]
    copies = [pltpu.make_async_copy(s, d, local_sem.at[i]) for i, (s, d) in enumerate(copies)]
    for copy in copies:
        copy.start()

    copies[0].wait()
    tokens = tokv[...].astype(F32)
    right = jnp.concatenate([tokens[HALF:], jnp.zeros((2 * HALF - TOK, 64), F32)], 0)
    block = jnp.concatenate([tokens[:HALF], right], 1).astype(BF16)
    pack[...] = block
    tok_all[me] = block
    pl.semaphore_wait(barrier, N - 1)

    def tok_copy(to):
        return pltpu.make_async_remote_copy(
            src_ref=pack, dst_ref=tok_all.at[me], send_sem=tok_send, recv_sem=tok_recv.at[me // 8],
            device_id=peer(to), device_id_type=MESH,
        )

    def tok_start(t, carry):
        tok_copy(lax.rem(me + step_of(t), N)).start()
        return carry

    lax.fori_loop(0, N - 1, tok_start, 0)

    for copy in copies[1:]:
        copy.wait()

    def begin(i, start):
        starts[i] = start
        return start + rows[i]

    lax.fori_loop(0, N, begin, 0)
    prepare(fv, b1v, gainv, b2v, me, ft, ft0, ghalf, b2col, place, xp)

    after = lax.rem(me + 1, N)

    def tok_wait(f, count):
        slabs = tok_all.at[pl.ds(0, count)]
        pltpu.make_async_remote_copy(
            src_ref=slabs, dst_ref=slabs, send_sem=tok_send, recv_sem=tok_recv.at[f], device_id=peer(after), device_id_type=MESH
        ).wait_recv()

    def out_copy(f, source, target, to):
        return pltpu.make_async_remote_copy(
            src_ref=source, dst_ref=target, send_sem=out_send.at[f], recv_sem=out_recv.at[f],
            device_id=peer(to), device_id_type=MESH,
        )

    for f, (send, recv) in enumerate(((send0, recv0), (send1, recv1))):
        @pl.when(me // 8 == f)
        def _():
            tok_wait(f, 7)

        @pl.when(me // 8 != f)
        def _():
            tok_wait(f, 8)

        patches(f, tok_all, place, xp)
        convolve(f, xp, ft, ft0, ghalf, wcat, hid, prod)
        gather_taps(f, me, prod, b2col, fin, rot)
        cut_strips(f, starts, fin, rot, send)

        def out_start(t, carry):
            to = lax.rem(me + step_of(t), N)
            out_copy(f, send.at[to], recv.at[me], to).start()
            return carry

        lax.fori_loop(0, N - 1, out_start, 0)
        recv[me] = send[me]

    pltpu.make_async_remote_copy(
        src_ref=tok_all.at[pl.ds(0, N - 1)], dst_ref=tok_all.at[pl.ds(0, N - 1)], send_sem=tok_send, recv_sem=tok_recv.at[0],
        device_id=peer(after), device_id_type=MESH,
    ).wait_send()
    for f, (send, recv) in enumerate(((send0, recv0), (send1, recv1))):
        out_copy(f, send.at[pl.ds(0, N - 1)], recv.at[pl.ds(0, N - 1)], after).wait()


def exchange(strip_rows, tokens, f, b1, gain, w, b2):
    hbm = pl.BlockSpec(memory_space=pltpu.HBM)
    return pl.pallas_call(
        main_kernel,
        out_shape=(pltpu.VMEM((N, CO, 128), BF16), pltpu.VMEM((N, CO + 8, 128), BF16)),
        in_specs=[hbm] * 7,
        out_specs=(pl.BlockSpec(memory_space=pltpu.VMEM),) * 2,
        scratch_shapes=[
            pltpu.SMEM((N,), jnp.int32),
            pltpu.VMEM((TOK, 64), BF16),
            pltpu.VMEM((2, 144, C2), BF16),
            pltpu.VMEM((1, C2), F32),
            pltpu.VMEM((1, C2), F32),
            pltpu.VMEM((1, C2), F32),
            pltpu.VMEM((HALF, 128), BF16),
            pltpu.VMEM((N, HALF, 128), BF16),
            pltpu.VMEM((C2, 304), BF16),
            pltpu.VMEM((C2, 160), BF16),
            pltpu.VMEM((C2, 128), F32),
            pltpu.VMEM((C2, 128), F32),
            pltpu.VMEM((2, 8 * HALF, FL), BF16),
            pltpu.VMEM((9 * CO, 2 * C2), BF16),
            pltpu.VMEM((304, 4 * FL), BF16),
            pltpu.VMEM((2 * C2, 4 * FL), BF16),
            pltpu.VMEM((9 * CO, 4 * FL), F32),
            pltpu.VMEM((FR, TILES, CO, 128), F32),
            pltpu.VMEM((FR, TILES, CO, 128), F32),
            pltpu.VMEM((N, CO, 128), BF16),
            pltpu.VMEM((N, CO + 8, 128), BF16),
            pltpu.SMEM((N,), jnp.int32),
            pltpu.SemaphoreType.DMA((9,)),
            pltpu.SemaphoreType.DMA,
            pltpu.SemaphoreType.DMA((FR,)),
            pltpu.SemaphoreType.DMA((FR,)),
            pltpu.SemaphoreType.DMA((FR,)),
        ],
        compiler_params=pltpu.CompilerParams(collective_id=0, has_side_effects=True, vmem_limit_bytes=40 << 20),
    )(*(pltpu.with_memory_space_constraint(v, pltpu.HBM) for v in (strip_rows, tokens, f, b1, gain, w, b2)))


def assemble_kernel(rows_ref, recv0, recv1, out):
    me = lax.axis_index("sp")

    def begin(i, start):
        return start + jnp.where(i < me, rows_ref[i], 0)

    start = lax.fori_loop(0, N, begin, 0)
    count = rows_ref[me]
    shape = (9 * 16, 256)
    p, lane = row_iota(shape), col_iota(shape)
    k, col = p // 16, p % 16
    row = (start + k) % 8
    at = row % 2 * 64 + col % 2 * 32 + row // 2 * PW + col // 2 + jnp.where(k == 8, 128, 0)
    pick = jnp.where((lane == at) & (k < count), 1.0, 0.0).astype(BF16)
    tail = recv1[...].astype(F32)[:, CO:]
    for f, recv in enumerate((recv0, recv1)):
        main = recv[...].astype(F32)[:, :CO].reshape(C2, 128)
        turns = [8 * m + 64 * f for m in range(3)]
        ninth = jnp.concatenate([pltpu.roll(tail, 128 - n, 2) if n else tail for n in turns], 1).reshape(C2, 128)
        both = jnp.concatenate([main, ninth], 1).astype(BF16)
        strip = lax.dot_general(pick, both, (((1,), (1,)), ((), ())), preferred_element_type=F32)
        out[0, f] = strip.astype(BF16).reshape(9, 16, C2)


def assemble(strip_rows, recv0, recv1):
    vmem = pl.BlockSpec(memory_space=pltpu.VMEM)
    return pl.pallas_call(
        assemble_kernel,
        out_shape=jax.ShapeDtypeStruct((1, FR, 9, 16, C2), BF16),
        in_specs=[pl.BlockSpec(memory_space=pltpu.SMEM), vmem, vmem],
        out_specs=vmem,
        compiler_params=pltpu.CompilerParams(vmem_limit_bytes=20 << 20),
    )(strip_rows, recv0, recv1)


def per_device(tokens, strip_rows, first_filter, first_bias, norm_gain, second_filter, second_bias):
    f = first_filter.reshape(3, 9 * C, C2)
    w = jnp.transpose(second_filter, (0, 1, 2, 4, 3)).reshape(3, 9 * CO, C2)
    recv0, recv1 = exchange(strip_rows, tokens, f, first_bias, norm_gain, w, second_bias)
    return assemble(strip_rows, recv0, recv1)


def solution(mesh):
    in_specs = (P(("req", "sp"), None), P(), P(), P(), P(), P(None, None, None, None, "sp"), P())
    out_specs = P(("req", "sp"), None, None, None, None)
    return jax.shard_map(
        per_device, mesh=mesh, in_specs=in_specs, out_specs=out_specs, check_vma=False
    )
```

time: 34.3 us -> 30 us (0.87)
  Pallas kernels: 34.1 us -> 29.1 us
  local copies, waits for them, and re-layouts: 0.01 us -> 0.65 us
    pallas_call x1, Pallas kernels: 32.5 us -> 27.5 us  [exchange(): pl.pallas_call(main_kernel, out_shape=(pltpu.VMEM((N, CO, 128), BF16), pl...]
    unnamed x2, local copies, waits for them, and re-layouts: 0.01 us -> 0.65 us
where the time goes in v3:
time: 30 us; the launch traced here: 29.8 us
  Pallas kernels  29.1 us (97%)
  local copies, waits for them, and re-layouts  0.65 us (2%)
    pallas_call x1, Pallas kernels, exchange(): pl.pallas_call(main_kernel, out_shape=(pltpu.VMEM((N, CO, 128), BF16), pl...  27.5 us
    pallas_call x1, Pallas kernels, assemble(): pl.pallas_call(assemble_kernel, out_shape=jax.ShapeDtypeStruct((1, FR, 9,...  1.69 us
    unnamed x2, local copies, waits for them, and re-layouts  0.65 us

profile of v3, /device:TPU:1, one launch (start us, length us, event | category | flops | bytes accessed | tf_op | source)
XLA Modules:
  0.0 29.8 jit_solution(5456930074957412722)
XLA Ops:
  0.0 27.5 %shard_map.73 = (bf16[16,24,128]{2,1,0:T(8,128)(2,1)S(1)}, bf16[16,32,128]{2,1,0:T(8,128)(2,1)S(1)}) custom-call(s32[16]{0:T(128)} %rows_ref.3, bf16[45,64]{1,0:T(8,128)(2,1)} %tok_ref.1, bf16[3,144,384]{2,1,0:T(8,128)(2,1)} %bitcast.5, f32[384]{0:T(512)} %b1_ref.1, f32[384]{0:T(512)} %gain_ref.1, bf16[3,216,384]{2,1,0:T(8,128)(2,1)} %bitcast.4, f32[384]{0:T(512)} %b2_ref.1), custom_call_target="tpu_custom_call" | custom-call | tf_op jit(solution)/shard_map/pallas_call | solution.py:287
  27.5 0.0 copy-start
  27.5 0.6 %copy-done = s32[16]{0:T(128)S(1)} copy-done((s32[16]{0:T(128)S(1)}, s32[16]{0:T(128)}, u32[]{:S(2)}) %copy-start) | copy-done | bytes 88
  28.1 1.7 %shard_map.74 = bf16[1,2,9,16,384]{4,3,2,1,0:T(8,128)(2,1)} custom-call(s32[16]{0:T(128)S(1)} %copy-done, bf16[16,24,128]{2,1,0:T(8,128)(2,1)S(1)} %get-tuple-element.7.recv0, bf16[16,32,128]{2,1,0:T(8,128)(2,1)S(1)} %get-tuple-element.8.recv1), custom_call_target="tpu_custom_call" | custom-call | tf_op jit(solution)/shard_map/pallas_call | solution.py:351
Async XLA Ops:
  27.5 0.7 %copy-start = (s32[16]{0:T(128)S(1)}, s32[16]{0:T(128)}, u32[]{:S(2)}) copy-start(s32[16]{0:T(128)} %rows_ref.3) | copy-start | bytes 196

commit v4 on v3

--- a/solution.py
+++ b/solution.py
@@ -10,6 +10,7 @@
 PH = 45
 PW = 8
 N = 16
+NF = N // FR
 TOK = FR * PH * PW // N
 HALF = 24
 FL = 384
@@ -26,9 +27,15 @@
     return {"sp": i}
 
 
-def step_of(t):
-    up = (t + 1) // 2
-    return 8 + up * (1 - 2 * ((t + 1) % 2))
+def for_others(me, low, high, act):
+    def step(i, carry):
+        @pl.when(i != me)
+        def _():
+            act(i)
+
+        return carry
+
+    lax.fori_loop(low, high, step, 0)
 
 
 def col_iota(shape):
@@ -186,19 +193,41 @@
         send[to] = jnp.concatenate([main, tail], 0).astype(BF16)
 
 
+def strip_pick(start, count):
+    shape = (9 * 16, 256)
+    p, lane = row_iota(shape), col_iota(shape)
+    k, col = p // 16, p % 16
+    row = (start + k) % 8
+    at = row % 2 * 64 + col % 2 * 32 + row // 2 * PW + col // 2 + jnp.where(k == 8, 128, 0)
+    return jnp.where((lane == at) & (k < count), 1.0, 0.0).astype(BF16)
+
+
 def main_kernel(
-    rows_ref, tok_ref, f_ref, b1_ref, gain_ref, w_ref, b2_ref, recv0, recv1,
+    rows_ref, tok_ref, f_ref, b1_ref, gain_ref, w_ref, b2_ref, recv0, recv1, pick,
     rows, tokv, fv, b1v, gainv, b2v, pack, tok_all, ft, ft0, ghalf, b2col, place, wcat, xp, hid, prod, fin, rot, send0, send1,
-    starts, local_sem, tok_send, tok_recv, out_send, out_recv,
+    starts, local_sem, go, tok_send, tok_recv, out_send, out_recv,
 ):
     me = lax.axis_index("sp")
+    early = me < NF
     barrier = pltpu.get_barrier_semaphore()
 
-    def greet(i, carry):
-        pl.semaphore_signal(barrier, inc=1, device_id=peer(lax.rem(me + i, N)), device_id_type=MESH)
-        return carry
-
-    lax.fori_loop(1, N, greet, 0)
+    def greet(i):
+        pl.semaphore_signal(barrier, inc=1, device_id=peer(i), device_id_type=MESH)
+
+    def tok_copy(to):
+        return pltpu.make_async_remote_copy(
+            src_ref=pack, dst_ref=tok_all.at[me], send_sem=tok_send, recv_sem=tok_recv.at[me // NF],
+            device_id=peer(to), device_id_type=MESH,
+        )
+
+    @pl.when(early)
+    def _():
+        for_others(me, 0, NF, greet)
+
+    @pl.when(jnp.logical_not(early))
+    def _():
+        pl.semaphore_wait(barrier, NF)
+        for_others(me, 0, NF, greet)
 
     copies = [
         (tok_ref, tokv), (f_ref.at[1], fv.at[0]), (f_ref.at[2], fv.at[1]), (b1_ref, b1v.at[0]), (gain_ref, gainv.at[0]), (b2_ref, b2v.at[0]),
@@ -214,19 +243,13 @@
     block = jnp.concatenate([tokens[:HALF], right], 1).astype(BF16)
     pack[...] = block
     tok_all[me] = block
-    pl.semaphore_wait(barrier, N - 1)
-
-    def tok_copy(to):
-        return pltpu.make_async_remote_copy(
-            src_ref=pack, dst_ref=tok_all.at[me], send_sem=tok_send, recv_sem=tok_recv.at[me // 8],
-            device_id=peer(to), device_id_type=MESH,
-        )
-
-    def tok_start(t, carry):
-        tok_copy(lax.rem(me + step_of(t), N)).start()
-        return carry
-
-    lax.fori_loop(0, N - 1, tok_start, 0)
+
+    @pl.when(early)
+    def _():
+        pl.semaphore_wait(barrier, NF - 1)
+        for_others(me, NF, N, greet)
+
+    for_others(me, 0, NF, lambda i: tok_copy(i).start())
 
     for copy in copies[1:]:
         copy.wait()
@@ -237,6 +260,18 @@
 
     lax.fori_loop(0, N, begin, 0)
     prepare(fv, b1v, gainv, b2v, me, ft, ft0, ghalf, b2col, place, xp)
+    pick[...] = strip_pick(starts[me], rows[me])
+
+    @pl.when(early)
+    def _():
+        pl.semaphore_wait(barrier, NF)
+        pl.semaphore_signal(go, inc=1, device_id=peer(me + NF), device_id_type=MESH)
+
+    @pl.when(jnp.logical_not(early))
+    def _():
+        pl.semaphore_wait(go, 1)
+
+    for_others(me, NF, N, lambda i: tok_copy(i).start())
 
     after = lax.rem(me + 1, N)
 
@@ -253,25 +288,20 @@
         )
 
     for f, (send, recv) in enumerate(((send0, recv0), (send1, recv1))):
-        @pl.when(me // 8 == f)
+        @pl.when(me // NF == f)
         def _():
-            tok_wait(f, 7)
-
-        @pl.when(me // 8 != f)
+            tok_wait(f, NF - 1)
+
+        @pl.when(me // NF != f)
         def _():
-            tok_wait(f, 8)
+            tok_wait(f, NF)
 
         patches(f, tok_all, place, xp)
         convolve(f, xp, ft, ft0, ghalf, wcat, hid, prod)
         gather_taps(f, me, prod, b2col, fin, rot)
         cut_strips(f, starts, fin, rot, send)
 
-        def out_start(t, carry):
-            to = lax.rem(me + step_of(t), N)
-            out_copy(f, send.at[to], recv.at[me], to).start()
-            return carry
-
-        lax.fori_loop(0, N - 1, out_start, 0)
+        for_others(me, 0, N, lambda to: out_copy(f, send.at[to], recv.at[me], to).start())
         recv[me] = send[me]
 
     pltpu.make_async_remote_copy(
@@ -286,9 +316,9 @@
     hbm = pl.BlockSpec(memory_space=pltpu.HBM)
     return pl.pallas_call(
         main_kernel,
-        out_shape=(pltpu.VMEM((N, CO, 128), BF16), pltpu.VMEM((N, CO + 8, 128), BF16)),
+        out_shape=(pltpu.VMEM((N, CO, 128), BF16), pltpu.VMEM((N, CO + 8, 128), BF16), pltpu.VMEM((9 * 16, 256), BF16)),
         in_specs=[hbm] * 7,
-        out_specs=(pl.BlockSpec(memory_space=pltpu.VMEM),) * 2,
+        out_specs=(pl.BlockSpec(memory_space=pltpu.VMEM),) * 3,
         scratch_shapes=[
             pltpu.SMEM((N,), jnp.int32),
             pltpu.VMEM((TOK, 64), BF16),
@@ -313,6 +343,7 @@
             pltpu.VMEM((N, CO + 8, 128), BF16),
             pltpu.SMEM((N,), jnp.int32),
             pltpu.SemaphoreType.DMA((9,)),
+            pltpu.SemaphoreType.REGULAR,
             pltpu.SemaphoreType.DMA,
             pltpu.SemaphoreType.DMA((FR,)),
             pltpu.SemaphoreType.DMA((FR,)),
@@ -322,46 +353,33 @@
     )(*(pltpu.with_memory_space_constraint(v, pltpu.HBM) for v in (strip_rows, tokens, f, b1, gain, w, b2)))
 
 
-def assemble_kernel(rows_ref, recv0, recv1, out):
-    me = lax.axis_index("sp")
-
-    def begin(i, start):
-        return start + jnp.where(i < me, rows_ref[i], 0)
-
-    start = lax.fori_loop(0, N, begin, 0)
-    count = rows_ref[me]
-    shape = (9 * 16, 256)
-    p, lane = row_iota(shape), col_iota(shape)
-    k, col = p // 16, p % 16
-    row = (start + k) % 8
-    at = row % 2 * 64 + col % 2 * 32 + row // 2 * PW + col // 2 + jnp.where(k == 8, 128, 0)
-    pick = jnp.where((lane == at) & (k < count), 1.0, 0.0).astype(BF16)
+def assemble_kernel(pick, recv0, recv1, out):
     tail = recv1[...].astype(F32)[:, CO:]
     for f, recv in enumerate((recv0, recv1)):
         main = recv[...].astype(F32)[:, :CO].reshape(C2, 128)
         turns = [8 * m + 64 * f for m in range(3)]
         ninth = jnp.concatenate([pltpu.roll(tail, 128 - n, 2) if n else tail for n in turns], 1).reshape(C2, 128)
         both = jnp.concatenate([main, ninth], 1).astype(BF16)
-        strip = lax.dot_general(pick, both, (((1,), (1,)), ((), ())), preferred_element_type=F32)
+        strip = lax.dot_general(pick[...], both, (((1,), (1,)), ((), ())), preferred_element_type=F32)
         out[0, f] = strip.astype(BF16).reshape(9, 16, C2)
 
 
-def assemble(strip_rows, recv0, recv1):
+def assemble(pick, recv0, recv1):
     vmem = pl.BlockSpec(memory_space=pltpu.VMEM)
     return pl.pallas_call(
         assemble_kernel,
         out_shape=jax.ShapeDtypeStruct((1, FR, 9, 16, C2), BF16),
-        in_specs=[pl.BlockSpec(memory_space=pltpu.SMEM), vmem, vmem],
+        in_specs=[vmem] * 3,
         out_specs=vmem,
         compiler_params=pltpu.CompilerParams(vmem_limit_bytes=20 << 20),
-    )(strip_rows, recv0, recv1)
+    )(pick, recv0, recv1)
 
 
 def per_device(tokens, strip_rows, first_filter, first_bias, norm_gain, second_filter, second_bias):
     f = first_filter.reshape(3, 9 * C, C2)
     w = jnp.transpose(second_filter, (0, 1, 2, 4, 3)).reshape(3, 9 * CO, C2)
-    recv0, recv1 = exchange(strip_rows, tokens, f, first_bias, norm_gain, w, second_bias)
-    return assemble(strip_rows, recv0, recv1)
+    recv0, recv1, pick = exchange(strip_rows, tokens, f, first_bias, norm_gain, w, second_bias)
+    return assemble(pick, recv0, recv1)
 
 
 def solution(mesh):

time: 30 us -> 30.8 us (1.027)
  Pallas kernels: 29.1 us -> 30.6 us
  local copies, waits for them, and re-layouts: 0.65 us -> 0 us
    pallas_call x1, Pallas kernels: 27.5 us -> 29.6 us  [exchange(): pl.pallas_call(main_kernel, out_shape=(pltpu.VMEM((N, CO, 128), BF16), pl...]
    pallas_call x1, Pallas kernels: 1.69 us -> 1.02 us  [assemble(): pl.pallas_call(assemble_kernel, out_shape=jax.ShapeDtypeStruct((1, FR, 9,...]
    unnamed x2 -> x0, local copies, waits for them, and re-layouts: 0.65 us -> none
where the time goes in v4:
time: 30.8 us; the launch traced here: 30.6 us
  Pallas kernels  30.6 us (99%)
    pallas_call x1, Pallas kernels, exchange(): pl.pallas_call(main_kernel, out_shape=(pltpu.VMEM((N, CO, 128), BF16), pl...  29.6 us
    pallas_call x1, Pallas kernels, assemble(): pl.pallas_call(assemble_kernel, out_shape=jax.ShapeDtypeStruct((1, FR, 9,...  1.02 us

profile of v4, /device:TPU:1, one launch (start us, length us, event | category | flops | bytes accessed | tf_op | source)
XLA Modules:
  0.0 30.6 jit_solution(5576404375939845056)
XLA Ops:
  0.0 29.6 %shard_map.73 = (bf16[16,24,128]{2,1,0:T(8,128)(2,1)S(1)}, bf16[16,32,128]{2,1,0:T(8,128)(2,1)S(1)}, bf16[144,256]{1,0:T(8,128)(2,1)S(1)}) custom-call(s32[16]{0:T(128)} %rows_ref.1, bf16[45,64]{1,0:T(8,128)(2,1)} %tok_ref.1, bf16[3,144,384]{2,1,0:T(8,128)(2,1)} %bitcast.5, f32[384]{0:T(512)} %b1_ref.1, f32[384]{0:T(512)} %gain_ref.1, ...), custom_call_target="tpu_custom_call" | custom-call | tf_op jit(solution)/shard_map/pallas_call | solution.py:317
  29.6 1.0 %shard_map.74 = bf16[1,2,9,16,384]{4,3,2,1,0:T(8,128)(2,1)} custom-call(bf16[144,256]{1,0:T(8,128)(2,1)S(1)} %get-tuple-element.8.pick, bf16[16,24,128]{2,1,0:T(8,128)(2,1)S(1)} %get-tuple-element.9.recv0, bf16[16,32,128]{2,1,0:T(8,128)(2,1)S(1)} %get-tuple-element.10.recv1), custom_call_target="tpu_custom_call" | custom-call | tf_op jit(solution)/shard_map/pallas_call | solution.py:369

commit v5 on v4

--- a/solution.py
+++ b/solution.py
@@ -205,7 +205,7 @@
 def main_kernel(
     rows_ref, tok_ref, f_ref, b1_ref, gain_ref, w_ref, b2_ref, recv0, recv1, pick,
     rows, tokv, fv, b1v, gainv, b2v, pack, tok_all, ft, ft0, ghalf, b2col, place, wcat, xp, hid, prod, fin, rot, send0, send1,
-    starts, local_sem, go, tok_send, tok_recv, out_send, out_recv,
+    starts, local_sem, ok, hub_send, tok_send, tok_recv, out_sent, out_recv,
 ):
     me = lax.axis_index("sp")
     early = me < NF
@@ -220,14 +220,21 @@
             device_id=peer(to), device_id_type=MESH,
         )
 
+    first_core = me % 2 == 0
+
     @pl.when(early)
     def _():
-        for_others(me, 0, NF, greet)
+        for chip in range(NF // 2):
+            @pl.when(me != 2 * chip)
+            def _():
+                greet(2 * chip)
+
+        for_others(me, NF, N, greet)
 
     @pl.when(jnp.logical_not(early))
     def _():
-        pl.semaphore_wait(barrier, NF)
-        for_others(me, 0, NF, greet)
+        greet(jnp.where(me < 10, 5, jnp.where(me < 12, 7, 1)))
+        for_others(me, NF, N, greet)
 
     copies = [
         (tok_ref, tokv), (f_ref.at[1], fv.at[0]), (f_ref.at[2], fv.at[1]), (b1_ref, b1v.at[0]), (gain_ref, gainv.at[0]), (b2_ref, b2v.at[0]),
@@ -244,12 +251,24 @@
     pack[...] = block
     tok_all[me] = block
 
+    @pl.when(early & first_core)
+    def _():
+        pl.semaphore_wait(barrier, NF - 1)
+        pl.semaphore_signal(ok, inc=1, device_id=peer(me + 1), device_id_type=MESH)
+
+    @pl.when(early & jnp.logical_not(first_core))
+    def _():
+        pl.semaphore_wait(ok, 1)
+
     @pl.when(early)
     def _():
-        pl.semaphore_wait(barrier, NF - 1)
-        for_others(me, NF, N, greet)
-
-    for_others(me, 0, NF, lambda i: tok_copy(i).start())
+        for_others(me, 0, NF, lambda i: tok_copy(i).start())
+
+    @pl.when(jnp.logical_not(early))
+    def _():
+        pl.semaphore_wait(barrier, N - 1)
+        for_others(me, NF, N, lambda i: tok_copy(i).start())
+        for_others(me, 0, NF, lambda i: tok_copy(i).start())
 
     for copy in copies[1:]:
         copy.wait()
@@ -261,17 +280,6 @@
     lax.fori_loop(0, N, begin, 0)
     prepare(fv, b1v, gainv, b2v, me, ft, ft0, ghalf, b2col, place, xp)
     pick[...] = strip_pick(starts[me], rows[me])
-
-    @pl.when(early)
-    def _():
-        pl.semaphore_wait(barrier, NF)
-        pl.semaphore_signal(go, inc=1, device_id=peer(me + NF), device_id_type=MESH)
-
-    @pl.when(jnp.logical_not(early))
-    def _():
-        pl.semaphore_wait(go, 1)
-
-    for_others(me, NF, N, lambda i: tok_copy(i).start())
 
     after = lax.rem(me + 1, N)
 
@@ -283,31 +291,89 @@
 
     def out_copy(f, source, target, to):
         return pltpu.make_async_remote_copy(
-            src_ref=source, dst_ref=target, send_sem=out_send.at[f], recv_sem=out_recv.at[f],
+            src_ref=source, dst_ref=target, send_sem=out_sent.at[f], recv_sem=out_recv.at[f],
             device_id=peer(to), device_id_type=MESH,
         )
 
+    def out_send(f, low, high):
+        send, recv = ((send0, recv0), (send1, recv1))[f]
+        for_others(me, low, high, lambda to: out_copy(f, send.at[to], recv.at[me], to).start())
+
+    def hub_copy(to):
+        slabs = tok_all.at[pl.ds(0, NF)]
+        return pltpu.make_async_remote_copy(
+            src_ref=slabs, dst_ref=slabs, send_sem=hub_send, recv_sem=tok_recv.at[0], device_id=peer(to), device_id_type=MESH
+        )
+
+    @pl.when(early)
+    def _():
+        tok_wait(0, NF - 1)
+
+    @pl.when(me == 1)
+    def _():
+        pl.semaphore_wait(barrier, 4)
+        for to in range(12, 16):
+            hub_copy(to).start()
+
+    @pl.when((me == 5) | (me == 7))
+    def _():
+        pl.semaphore_wait(barrier, 2)
+        hub_copy(me + 3).start()
+        hub_copy(me + 4).start()
+
     for f, (send, recv) in enumerate(((send0, recv0), (send1, recv1))):
-        @pl.when(me // NF == f)
-        def _():
-            tok_wait(f, NF - 1)
-
-        @pl.when(me // NF != f)
-        def _():
-            tok_wait(f, NF)
+        if f == 0:
+            @pl.when(jnp.logical_not(early))
+            def _():
+                tok_wait(0, NF)
+        else:
+            @pl.when(early)
+            def _():
+                tok_wait(1, NF)
+                out_send(0, NF, N)
+
+            @pl.when(jnp.logical_not(early))
+            def _():
+                tok_wait(1, NF - 1)
 
         patches(f, tok_all, place, xp)
         convolve(f, xp, ft, ft0, ghalf, wcat, hid, prod)
         gather_taps(f, me, prod, b2col, fin, rot)
         cut_strips(f, starts, fin, rot, send)
 
-        for_others(me, 0, N, lambda to: out_copy(f, send.at[to], recv.at[me], to).start())
+        if f == 0:
+            out_send(0, 0, NF)
+
+            @pl.when(jnp.logical_not(early))
+            def _():
+                out_send(0, NF, N)
+        else:
+            out_send(1, 0, N)
         recv[me] = send[me]
 
-    pltpu.make_async_remote_copy(
-        src_ref=tok_all.at[pl.ds(0, N - 1)], dst_ref=tok_all.at[pl.ds(0, N - 1)], send_sem=tok_send, recv_sem=tok_recv.at[0],
-        device_id=peer(after), device_id_type=MESH,
-    ).wait_send()
+    def tok_sent(count, sem):
+        slabs = tok_all.at[pl.ds(0, count)]
+        pltpu.make_async_remote_copy(
+            src_ref=slabs, dst_ref=slabs, send_sem=sem, recv_sem=tok_recv.at[0], device_id=peer(after), device_id_type=MESH
+        ).wait_send()
+
+    @pl.when(early)
+    def _():
+        tok_sent(NF - 1, tok_send)
+
+    @pl.when(jnp.logical_not(early))
+    def _():
+        tok_sent(N - 1, tok_send)
+
+    @pl.when(me == 1)
+    def _():
+        tok_sent(N, hub_send)
+        tok_sent(N, hub_send)
+
+    @pl.when((me == 5) | (me == 7))
+    def _():
+        tok_sent(N, hub_send)
+
     for f, (send, recv) in enumerate(((send0, recv0), (send1, recv1))):
         out_copy(f, send.at[pl.ds(0, N - 1)], recv.at[pl.ds(0, N - 1)], after).wait()
 
@@ -345,6 +411,7 @@
             pltpu.SemaphoreType.DMA((9,)),
             pltpu.SemaphoreType.REGULAR,
             pltpu.SemaphoreType.DMA,
+            pltpu.SemaphoreType.DMA,
             pltpu.SemaphoreType.DMA((FR,)),
             pltpu.SemaphoreType.DMA((FR,)),
             pltpu.SemaphoreType.DMA((FR,)),

time: 30.8 us -> 27.3 us (0.89)
  Pallas kernels: 30.6 us -> 27.1 us
    pallas_call x1, Pallas kernels: 29.6 us -> 26.1 us  [exchange(): pl.pallas_call(main_kernel, out_shape=(pltpu.VMEM((N, CO, 128), BF16), pl...]
where the time goes in v5:
time: 27.3 us; the launch traced here: 27.1 us
  Pallas kernels  27.1 us (99%)
    pallas_call x1, Pallas kernels, exchange(): pl.pallas_call(main_kernel, out_shape=(pltpu.VMEM((N, CO, 128), BF16), pl...  26.1 us
    pallas_call x1, Pallas kernels, assemble(): pl.pallas_call(assemble_kernel, out_shape=jax.ShapeDtypeStruct((1, FR, 9,...  1.02 us

profile of v5, /device:TPU:1, one launch (start us, length us, event | category | flops | bytes accessed | tf_op | source)
XLA Modules:
  0.0 27.1 jit_solution(9974014984389125124)
XLA Ops:
  0.0 26.1 %shard_map.73 = (bf16[16,24,128]{2,1,0:T(8,128)(2,1)S(1)}, bf16[16,32,128]{2,1,0:T(8,128)(2,1)S(1)}, bf16[144,256]{1,0:T(8,128)(2,1)S(1)}) custom-call(s32[16]{0:T(128)} %rows_ref.1, bf16[45,64]{1,0:T(8,128)(2,1)} %tok_ref.1, bf16[3,144,384]{2,1,0:T(8,128)(2,1)} %bitcast.5, f32[384]{0:T(512)} %b1_ref.1, f32[384]{0:T(512)} %gain_ref.1, ...), custom_call_target="tpu_custom_call" | custom-call | tf_op jit(solution)/shard_map/pallas_call | solution.py:383
  26.1 1.0 %shard_map.74 = bf16[1,2,9,16,384]{4,3,2,1,0:T(8,128)(2,1)} custom-call(bf16[144,256]{1,0:T(8,128)(2,1)S(1)} %get-tuple-element.8.pick, bf16[16,24,128]{2,1,0:T(8,128)(2,1)S(1)} %get-tuple-element.9.recv0, bf16[16,32,128]{2,1,0:T(8,128)(2,1)S(1)} %get-tuple-element.10.recv1), custom_call_target="tpu_custom_call" | custom-call | tf_op jit(solution)/shard_map/pallas_call | solution.py:436

commit v6 on v5

--- a/solution.py
+++ b/solution.py
@@ -11,6 +11,7 @@
 PW = 8
 N = 16
 NF = N // FR
+FIRST = 8
 TOK = FR * PH * PW // N
 HALF = 24
 FL = 384
@@ -102,7 +103,7 @@
                                 xp[row:row + C, ph * FL:(ph + 1) * FL] = moved[sr, sq]
 
 
-def convolve(f, xp, ft, ft0, ghalf, wcat, hid, prod):
+def convolve(f, xp, ft, ft0, ghalf, wcat, hid, prod, between=None):
     def first_of(at):
         lanes = slice(at, at + CHUNK)
         if f == 0:
@@ -112,9 +113,9 @@
     def second_of(at):
         lanes = slice(at, at + CHUNK)
         if f == 0:
-            prod[:, lanes] = jnp.dot(wcat[:, C2:], hid[0:C2, lanes], preferred_element_type=F32)
+            prod[f, :, lanes] = jnp.dot(wcat[:, C2:], hid[0:C2, lanes], preferred_element_type=F32)
         else:
-            prod[:, lanes] = jnp.dot(wcat[...], hid[:, lanes], preferred_element_type=F32)
+            prod[f, :, lanes] = jnp.dot(wcat[...], hid[:, lanes], preferred_element_type=F32)
 
     def act(at, first):
         lanes = slice(at, at + CHUNK)
@@ -132,6 +133,8 @@
         act(at, ready)
         if n:
             second_of(ats[n - 1])
+        if between is not None and n == 1:
+            between()
         ready = ahead
     second_of(ats[-1])
 
@@ -149,7 +152,7 @@
                     sa, sr = shift_of(a, dy - 1)
                     sb, sq = shift_of(b, dx - 1)
                     tap, ph = dy * 3 + dx, sa * 2 + sb
-                    term = prod[tap * CO:(tap + 1) * CO, ph * FL:(ph + 1) * FL]
+                    term = prod[f, tap * CO:(tap + 1) * CO, ph * FL:(ph + 1) * FL]
                     sums[sr, sq] = sums[sr, sq] + term if (sr, sq) in sums else term
             sr, sq = (-1, 1)[a], (-1, 1)[b]
             side = sums[0, sq] + pltpu.roll(sums[sr, sq], (-PW * sr) % FL, 1)
@@ -173,24 +176,36 @@
     rot[f, TILES - 1] = jnp.zeros((CO, 128), F32)
 
 
-def cut_strips(f, starts, fin, rot, send):
-    lane = col_iota((1, 128))
-    row = (lane % 32) // PW * 2 + lane // 64
+def mask_strips(rows, starts, tiles, keep, slots):
+    lane = col_iota((8, 128))
+    row = ((lane & 31) >> 3) * 2 + (lane >> 6)
+
+    def step(to, start):
+        off = start & 7
+        starts[to] = start
+        tiles[to] = start >> 3
+        keep[to] = (row >= off).astype(jnp.int32)
+        slot = ((lane >> 3) + 16 - ((off & 1) * 8 + (off >> 1))) & 15
+        slots[to] = (slot >> 3) * 3 + (slot & 3)
+        return start + rows[to]
+
+    lax.fori_loop(0, N, step, 0)
+
+
+def cut_strips(f, tiles, keep, slots, fin, rot, send):
     for to in range(N):
-        start = starts[to]
-        tile, off = start // 8, start % 8
-        main = jnp.where(row >= off, fin[f, tile], fin[f, tile + 1])
-        if f == 0:
-            send[to] = main.astype(BF16)
-            continue
-        slot = (lane // 8 + 16 - (off % 2 * 8 + off // 2)) % 16
-        tail = None
-        for g in range(FR):
-            ninth = rot[g, tile + 1]
-            for m in range(3):
-                part = ninth[8 * m:8 * m + 8]
-                tail = part if tail is None else jnp.where((slot // 8 == g) & (slot % 4 == m), part, tail)
-        send[to] = jnp.concatenate([main, tail], 0).astype(BF16)
+        tile = tiles[to]
+        first = keep[to] > 0
+        one, two = fin[f, tile], fin[f, tile + 1]
+        parts = [jnp.where(first, one[8 * m:8 * m + 8], two[8 * m:8 * m + 8]) for m in range(3)]
+        if f == 1:
+            slot = slots[to]
+            tail = rot[0, tile + 1][:8]
+            for n in range(1, 6):
+                m = n % 3
+                tail = jnp.where(slot == n, rot[n // 3, tile + 1][8 * m:8 * m + 8], tail)
+            parts.append(tail)
+        send[to] = jnp.concatenate(parts, 0).astype(BF16)
 
 
 def strip_pick(start, count):
@@ -205,7 +220,7 @@
 def main_kernel(
     rows_ref, tok_ref, f_ref, b1_ref, gain_ref, w_ref, b2_ref, recv0, recv1, pick,
     rows, tokv, fv, b1v, gainv, b2v, pack, tok_all, ft, ft0, ghalf, b2col, place, wcat, xp, hid, prod, fin, rot, send0, send1,
-    starts, local_sem, ok, hub_send, tok_send, tok_recv, out_sent, out_recv,
+    starts, tiles, keep, slots, local_sem, ok, hub_send, tok_send, tok_recv, out_sent, out_recv,
 ):
     me = lax.axis_index("sp")
     early = me < NF
@@ -216,7 +231,7 @@
 
     def tok_copy(to):
         return pltpu.make_async_remote_copy(
-            src_ref=pack, dst_ref=tok_all.at[me], send_sem=tok_send, recv_sem=tok_recv.at[me // NF],
+            src_ref=pack, dst_ref=tok_all.at[me], send_sem=tok_send, recv_sem=tok_recv.at[jnp.minimum(me // 2, 4)],
             device_id=peer(to), device_id_type=MESH,
         )
 
@@ -273,11 +288,7 @@
     for copy in copies[1:]:
         copy.wait()
 
-    def begin(i, start):
-        starts[i] = start
-        return start + rows[i]
-
-    lax.fori_loop(0, N, begin, 0)
+    mask_strips(rows, starts, tiles, keep, slots)
     prepare(fv, b1v, gainv, b2v, me, ft, ft0, ghalf, b2col, place, xp)
     pick[...] = strip_pick(starts[me], rows[me])
 
@@ -295,61 +306,96 @@
             device_id=peer(to), device_id_type=MESH,
         )
 
-    def out_send(f, low, high):
+    def out_start(f, i):
         send, recv = ((send0, recv0), (send1, recv1))[f]
-        for_others(me, low, high, lambda to: out_copy(f, send.at[to], recv.at[me], to).start())
-
-    def hub_copy(to):
-        slabs = tok_all.at[pl.ds(0, NF)]
-        return pltpu.make_async_remote_copy(
-            src_ref=slabs, dst_ref=slabs, send_sem=hub_send, recv_sem=tok_recv.at[0], device_id=peer(to), device_id_type=MESH
-        )
+        twin = me + 1 - 2 * (me % 2)
+        at = i + (i >= twin).astype(jnp.int32)
+        to = at + 1 - 2 * (at % 2)
+        out_copy(f, send.at[to], recv.at[me], to).start()
+
+    def finish(f):
+        send, recv = ((send0, recv0), (send1, recv1))[f]
+        gather_taps(f, me, prod, b2col, fin, rot)
+        cut_strips(f, tiles, keep, slots, fin, rot, send)
+        for i in range(N - 1):
+            if f == 1 and i >= FIRST:
+                out_start(0, i)
+            if f == 1 or i < FIRST:
+                out_start(f, i)
+        recv[me] = send[me]
+
+    def hub_pass(clients, low, high):
+        slabs = tok_all.at[pl.ds(low, high - low)]
+        for to in clients:
+            pltpu.make_async_remote_copy(
+                src_ref=slabs, dst_ref=slabs, send_sem=hub_send, recv_sem=tok_recv.at[0], device_id=peer(to), device_id_type=MESH
+            ).start()
+
+    @pl.when(me == 1)
+    def _():
+        clients = range(12, 16)
+        tok_wait(0, 1)
+        tok_wait(1, 2)
+        pl.semaphore_wait(barrier, 4)
+        hub_pass(clients, 0, 4)
+        tok_wait(2, 2)
+        hub_pass(clients, 4, 6)
+        tok_wait(3, 2)
+        hub_pass(clients, 6, 8)
+
+    @pl.when(me == 5)
+    def _():
+        clients = (8, 9)
+        tok_wait(2, 1)
+        tok_wait(1, 2)
+        pl.semaphore_wait(barrier, 2)
+        hub_pass(clients, 2, 6)
+        tok_wait(3, 2)
+        hub_pass(clients, 6, 8)
+        tok_wait(0, 2)
+        hub_pass(clients, 0, 2)
+
+    @pl.when(me == 7)
+    def _():
+        clients = (10, 11)
+        tok_wait(3, 1)
+        tok_wait(2, 2)
+        pl.semaphore_wait(barrier, 2)
+        hub_pass(clients, 4, 8)
+        tok_wait(1, 2)
+        hub_pass(clients, 2, 4)
+        tok_wait(0, 2)
+        hub_pass(clients, 0, 2)
+
+    @pl.when(early & (first_core | (me == 3)))
+    def _():
+        for chip in range(4):
+            @pl.when(me // 2 == chip)
+            def _():
+                tok_wait(chip, 1)
+
+            @pl.when(me // 2 != chip)
+            def _():
+                tok_wait(chip, 2)
+
+    @pl.when(jnp.logical_not(early))
+    def _():
+        tok_wait(0, NF)
+
+    patches(0, tok_all, place, xp)
+    convolve(0, xp, ft, ft0, ghalf, wcat, hid, prod)
 
     @pl.when(early)
     def _():
-        tok_wait(0, NF - 1)
-
-    @pl.when(me == 1)
-    def _():
-        pl.semaphore_wait(barrier, 4)
-        for to in range(12, 16):
-            hub_copy(to).start()
-
-    @pl.when((me == 5) | (me == 7))
-    def _():
-        pl.semaphore_wait(barrier, 2)
-        hub_copy(me + 3).start()
-        hub_copy(me + 4).start()
-
-    for f, (send, recv) in enumerate(((send0, recv0), (send1, recv1))):
-        if f == 0:
-            @pl.when(jnp.logical_not(early))
-            def _():
-                tok_wait(0, NF)
-        else:
-            @pl.when(early)
-            def _():
-                tok_wait(1, NF)
-                out_send(0, NF, N)
-
-            @pl.when(jnp.logical_not(early))
-            def _():
-                tok_wait(1, NF - 1)
-
-        patches(f, tok_all, place, xp)
-        convolve(f, xp, ft, ft0, ghalf, wcat, hid, prod)
-        gather_taps(f, me, prod, b2col, fin, rot)
-        cut_strips(f, starts, fin, rot, send)
-
-        if f == 0:
-            out_send(0, 0, NF)
-
-            @pl.when(jnp.logical_not(early))
-            def _():
-                out_send(0, NF, N)
-        else:
-            out_send(1, 0, N)
-        recv[me] = send[me]
+        tok_wait(4, NF)
+
+    @pl.when(jnp.logical_not(early))
+    def _():
+        tok_wait(4, NF - 1)
+
+    patches(1, tok_all, place, xp)
+    convolve(1, xp, ft, ft0, ghalf, wcat, hid, prod, lambda: finish(0))
+    finish(1)
 
     def tok_sent(count, sem):
         slabs = tok_all.at[pl.ds(0, count)]
@@ -402,17 +448,20 @@
             pltpu.VMEM((9 * CO, 2 * C2), BF16),
             pltpu.VMEM((304, 4 * FL), BF16),
             pltpu.VMEM((2 * C2, 4 * FL), BF16),
-            pltpu.VMEM((9 * CO, 4 * FL), F32),
+            pltpu.VMEM((FR, 9 * CO, 4 * FL), F32),
             pltpu.VMEM((FR, TILES, CO, 128), F32),
             pltpu.VMEM((FR, TILES, CO, 128), F32),
             pltpu.VMEM((N, CO, 128), BF16),
             pltpu.VMEM((N, CO + 8, 128), BF16),
             pltpu.SMEM((N,), jnp.int32),
+            pltpu.SMEM((N,), jnp.int32),
+            pltpu.VMEM((N, 8, 128), jnp.int32),
+            pltpu.VMEM((N, 8, 128), jnp.int32),
             pltpu.SemaphoreType.DMA((9,)),
             pltpu.SemaphoreType.REGULAR,
             pltpu.SemaphoreType.DMA,
             pltpu.SemaphoreType.DMA,
-            pltpu.SemaphoreType.DMA((FR,)),
+            pltpu.SemaphoreType.DMA((5,)),
             pltpu.SemaphoreType.DMA((FR,)),
             pltpu.SemaphoreType.DMA((FR,)),
         ],
@@ -420,15 +469,20 @@
     )(*(pltpu.with_memory_space_constraint(v, pltpu.HBM) for v in (strip_rows, tokens, f, b1, gain, w, b2)))
 
 
-def assemble_kernel(pick, recv0, recv1, out):
+def assemble_kernel(pick, recv0, recv1, out, strips, sent):
     tail = recv1[...].astype(F32)[:, CO:]
+    copies = []
     for f, recv in enumerate((recv0, recv1)):
         main = recv[...].astype(F32)[:, :CO].reshape(C2, 128)
         turns = [8 * m + 64 * f for m in range(3)]
         ninth = jnp.concatenate([pltpu.roll(tail, 128 - n, 2) if n else tail for n in turns], 1).reshape(C2, 128)
         both = jnp.concatenate([main, ninth], 1).astype(BF16)
         strip = lax.dot_general(pick[...], both, (((1,), (1,)), ((), ())), preferred_element_type=F32)
-        out[0, f] = strip.astype(BF16).reshape(9, 16, C2)
+        strips[f] = strip.astype(BF16).reshape(9, 16, C2)
+        copies.append(pltpu.make_async_copy(strips.at[f], out.at[0, f], sent.at[f]))
+        copies[f].start()
+    for copy in copies:
+        copy.wait()
 
 
 def assemble(pick, recv0, recv1):
@@ -437,7 +491,8 @@
         assemble_kernel,
         out_shape=jax.ShapeDtypeStruct((1, FR, 9, 16, C2), BF16),
         in_specs=[vmem] * 3,
-        out_specs=vmem,
+        out_specs=pl.BlockSpec(memory_space=pl.ANY),
+        scratch_shapes=[pltpu.VMEM((FR, 9, 16, C2), BF16), pltpu.SemaphoreType.DMA((FR,))],
         compiler_params=pltpu.CompilerParams(vmem_limit_bytes=20 << 20),
     )(pick, recv0, recv1)
 

time: 27.3 us -> 26.7 us (0.978)
  Pallas kernels: 27.1 us -> 26.6 us
    pallas_call x1, Pallas kernels: 26.1 us -> 25.6 us  [exchange(): pl.pallas_call(main_kernel, out_shape=(pltpu.VMEM((N, CO, 128), BF16), pl...]
where the time goes in v6:
time: 26.7 us; the launch traced here: 26.6 us
  Pallas kernels  26.6 us (100%)
    pallas_call x1, Pallas kernels, exchange(): pl.pallas_call(main_kernel, out_shape=(pltpu.VMEM((N, CO, 128), BF16), pl...  25.6 us
    pallas_call x1, Pallas kernels, assemble(): pl.pallas_call(assemble_kernel, out_shape=jax.ShapeDtypeStruct((1, FR, 9,...  0.99 us

profile of v6, /device:TPU:1, one launch (start us, length us, event | category | flops | bytes accessed | tf_op | source)
XLA Modules:
  0.0 26.6 jit_solution(1741597438730267310)
XLA Ops:
  0.0 25.6 %shard_map.73 = (bf16[16,24,128]{2,1,0:T(8,128)(2,1)S(1)}, bf16[16,32,128]{2,1,0:T(8,128)(2,1)S(1)}, bf16[144,256]{1,0:T(8,128)(2,1)S(1)}) custom-call(s32[16]{0:T(128)} %rows_ref.1, bf16[45,64]{1,0:T(8,128)(2,1)} %tok_ref.1, bf16[3,144,384]{2,1,0:T(8,128)(2,1)} %bitcast.5, f32[384]{0:T(512)} %b1_ref.1, f32[384]{0:T(512)} %gain_ref.1, ...), custom_call_target="tpu_custom_call" | custom-call | tf_op jit(solution)/shard_map/pallas_call | solution.py:429
  25.6 1.0 %shard_map.74 = bf16[1,2,9,16,384]{4,3,2,1,0:T(8,128)(2,1)} custom-call(bf16[144,256]{1,0:T(8,128)(2,1)S(1)} %get-tuple-element.8.pick, bf16[16,24,128]{2,1,0:T(8,128)(2,1)S(1)} %get-tuple-element.9.recv0, bf16[16,32,128]{2,1,0:T(8,128)(2,1)S(1)} %get-tuple-element.10.recv1), custom_call_target="tpu_custom_call" | custom-call | tf_op jit(solution)/shard_map/pallas_call | solution.py:490

commit v7 on v6

--- a/solution.py
+++ b/solution.py
@@ -11,7 +11,7 @@
 PW = 8
 N = 16
 NF = N // FR
-FIRST = 8
+FIRST = 4
 TOK = FR * PH * PW // N
 HALF = 24
 FL = 384
@@ -52,7 +52,7 @@
     return moved % 2, moved // 2
 
 
-def prepare(f_ref, b1_ref, gain_ref, b2_ref, me, ft, ft0, ghalf, b2col, place, xp):
+def prepare(f_ref, b1_ref, gain_ref, b2_ref, me, now, back, ghalf, b2col, place, xp):
     tap1, tap2 = f_ref[0].astype(F32), f_ref[1].astype(F32)
     bias = b1_ref[...]
     hi = bias.astype(BF16).astype(F32)
@@ -60,8 +60,8 @@
     low = bias - hi - mid
     rows = row_iota((16, C2))
     bias_rows = jnp.where(rows == 0, hi, jnp.where(rows == 1, mid, jnp.where(rows == 2, low, 0.0)))
-    ft[...] = jnp.concatenate([tap2, bias_rows, tap1, jnp.zeros((80, C2), F32)], 0).T[:, :304].astype(BF16)
-    ft0[...] = jnp.concatenate([bias_rows, tap2, jnp.zeros((96, C2), F32)], 0).T[:, :160].astype(BF16)
+    now[...] = jnp.concatenate([tap2, bias_rows, jnp.zeros((96, C2), F32)], 0).T[:, :160].astype(BF16)
+    back[...] = jnp.concatenate([tap1, jnp.zeros((112, C2), F32)], 0).T[:, :144].astype(BF16)
     ghalf[...] = jnp.broadcast_to(gain_ref[...] * 0.5, (128, C2)).T
     b2col[...] = jnp.broadcast_to(b2_ref[...], (128, C2)).T
     shape = (8 * HALF, FL)
@@ -72,6 +72,7 @@
     place[0] = jnp.where(lane == src * TOK + i, one, zero).astype(BF16)
     place[1] = jnp.where((lane == src * TOK + HALF + i) & (i < TOK - HALF), one, zero).astype(BF16)
     xp[144:160, :] = jnp.ones((16, 4 * FL), BF16)
+    xp[304:320, :] = jnp.ones((16, 4 * FL), BF16)
 
 
 def patches(f, tok_all, place, xp):
@@ -103,12 +104,17 @@
                                 xp[row:row + C, ph * FL:(ph + 1) * FL] = moved[sr, sq]
 
 
-def convolve(f, xp, ft, ft0, ghalf, wcat, hid, prod, between=None):
+def convolve_own(xp, now, own):
+    for at in range(0, 4 * FL, CHUNK):
+        own[:, at:at + CHUNK] = jnp.dot(now[...], xp[0:160, at:at + CHUNK], preferred_element_type=F32)
+
+
+def convolve(f, xp, now, back, own, ghalf, wcat, hid, prod, between=None):
     def first_of(at):
         lanes = slice(at, at + CHUNK)
         if f == 0:
-            return jnp.dot(ft0[...], xp[144:304, lanes], preferred_element_type=F32)
-        return jnp.dot(ft[...], xp[:, lanes], preferred_element_type=F32)
+            return jnp.dot(now[...], xp[160:320, lanes], preferred_element_type=F32)
+        return jnp.dot(back[...], xp[160:304, lanes], preferred_element_type=F32) + own[:, lanes]
 
     def second_of(at):
         lanes = slice(at, at + CHUNK)
@@ -192,20 +198,19 @@
     lax.fori_loop(0, N, step, 0)
 
 
-def cut_strips(f, tiles, keep, slots, fin, rot, send):
-    for to in range(N):
-        tile = tiles[to]
-        first = keep[to] > 0
-        one, two = fin[f, tile], fin[f, tile + 1]
-        parts = [jnp.where(first, one[8 * m:8 * m + 8], two[8 * m:8 * m + 8]) for m in range(3)]
-        if f == 1:
-            slot = slots[to]
-            tail = rot[0, tile + 1][:8]
-            for n in range(1, 6):
-                m = n % 3
-                tail = jnp.where(slot == n, rot[n // 3, tile + 1][8 * m:8 * m + 8], tail)
-            parts.append(tail)
-        send[to] = jnp.concatenate(parts, 0).astype(BF16)
+def cut_strip(f, to, tiles, keep, slots, fin, rot):
+    tile = tiles[to]
+    first = keep[to] > 0
+    one, two = fin[f, tile], fin[f, tile + 1]
+    parts = [jnp.where(first, one[8 * m:8 * m + 8], two[8 * m:8 * m + 8]) for m in range(3)]
+    if f == 1:
+        slot = slots[to]
+        tail = rot[0, tile + 1][:8]
+        for n in range(1, 6):
+            m = n % 3
+            tail = jnp.where(slot == n, rot[n // 3, tile + 1][8 * m:8 * m + 8], tail)
+        parts.append(tail)
+    return jnp.concatenate(parts, 0).astype(BF16)
 
 
 def strip_pick(start, count):
@@ -219,7 +224,7 @@
 
 def main_kernel(
     rows_ref, tok_ref, f_ref, b1_ref, gain_ref, w_ref, b2_ref, recv0, recv1, pick,
-    rows, tokv, fv, b1v, gainv, b2v, pack, tok_all, ft, ft0, ghalf, b2col, place, wcat, xp, hid, prod, fin, rot, send0, send1,
+    rows, tokv, fv, b1v, gainv, b2v, pack, tok_all, now, back, ghalf, b2col, place, wcat, xp, own, hid, prod, fin, rot, send0, send1,
     starts, tiles, keep, slots, local_sem, ok, hub_send, tok_send, tok_recv, out_sent, out_recv,
 ):
     me = lax.axis_index("sp")
@@ -236,6 +241,8 @@
         )
 
     first_core = me % 2 == 0
+    tok_fetch = pltpu.make_async_copy(tok_ref, tokv, local_sem.at[0])
+    tok_fetch.start()
 
     @pl.when(early)
     def _():
@@ -252,14 +259,14 @@
         for_others(me, NF, N, greet)
 
     copies = [
-        (tok_ref, tokv), (f_ref.at[1], fv.at[0]), (f_ref.at[2], fv.at[1]), (b1_ref, b1v.at[0]), (gain_ref, gainv.at[0]), (b2_ref, b2v.at[0]),
+        (f_ref.at[1], fv.at[0]), (f_ref.at[2], fv.at[1]), (b1_ref, b1v.at[0]), (gain_ref, gainv.at[0]), (b2_ref, b2v.at[0]),
         (w_ref.at[1], wcat.at[:, 0:C2]), (w_ref.at[2], wcat.at[:, C2:2 * C2]), (rows_ref, rows),
     ]
-    copies = [pltpu.make_async_copy(s, d, local_sem.at[i]) for i, (s, d) in enumerate(copies)]
+    copies = [pltpu.make_async_copy(s, d, local_sem.at[i + 1]) for i, (s, d) in enumerate(copies)]
     for copy in copies:
         copy.start()
 
-    copies[0].wait()
+    tok_fetch.wait()
     tokens = tokv[...].astype(F32)
     right = jnp.concatenate([tokens[HALF:], jnp.zeros((2 * HALF - TOK, 64), F32)], 0)
     block = jnp.concatenate([tokens[:HALF], right], 1).astype(BF16)
@@ -275,7 +282,11 @@
     def _():
         pl.semaphore_wait(ok, 1)
 
-    @pl.when(early)
+    @pl.when(me < 4)
+    def _():
+        for_others(NF - 1 - me, 0, NF, lambda i: tok_copy(NF - 1 - i).start())
+
+    @pl.when((me >= 4) & early)
     def _():
         for_others(me, 0, NF, lambda i: tok_copy(i).start())
 
@@ -285,11 +296,11 @@
         for_others(me, NF, N, lambda i: tok_copy(i).start())
         for_others(me, 0, NF, lambda i: tok_copy(i).start())
 
-    for copy in copies[1:]:
+    for copy in copies:
         copy.wait()
 
     mask_strips(rows, starts, tiles, keep, slots)
-    prepare(fv, b1v, gainv, b2v, me, ft, ft0, ghalf, b2col, place, xp)
+    prepare(fv, b1v, gainv, b2v, me, now, back, ghalf, b2col, place, xp)
     pick[...] = strip_pick(starts[me], rows[me])
 
     after = lax.rem(me + 1, N)
@@ -306,66 +317,68 @@
             device_id=peer(to), device_id_type=MESH,
         )
 
+    def other(i):
+        twin = me + 1 - 2 * (me % 2)
+        at = i + (i >= twin).astype(jnp.int32)
+        return at + 1 - 2 * (at % 2)
+
     def out_start(f, i):
         send, recv = ((send0, recv0), (send1, recv1))[f]
-        twin = me + 1 - 2 * (me % 2)
-        at = i + (i >= twin).astype(jnp.int32)
-        to = at + 1 - 2 * (at % 2)
+        to = other(i)
         out_copy(f, send.at[to], recv.at[me], to).start()
 
     def finish(f):
         send, recv = ((send0, recv0), (send1, recv1))[f]
         gather_taps(f, me, prod, b2col, fin, rot)
-        cut_strips(f, tiles, keep, slots, fin, rot, send)
         for i in range(N - 1):
+            to = other(i)
+            send[to] = cut_strip(f, to, tiles, keep, slots, fin, rot)
             if f == 1 and i >= FIRST:
                 out_start(0, i)
             if f == 1 or i < FIRST:
                 out_start(f, i)
-        recv[me] = send[me]
-
-    def hub_pass(clients, low, high):
-        slabs = tok_all.at[pl.ds(low, high - low)]
+        recv[me] = cut_strip(f, me, tiles, keep, slots, fin, rot)
+
+    def hub_pass(clients, low, which):
+        slabs = tok_all.at[pl.ds(low, 4 - 2 * which)]
         for to in clients:
             pltpu.make_async_remote_copy(
-                src_ref=slabs, dst_ref=slabs, send_sem=hub_send, recv_sem=tok_recv.at[0], device_id=peer(to), device_id_type=MESH
+                src_ref=slabs, dst_ref=slabs, send_sem=hub_send, recv_sem=tok_recv.at[1 - which],
+                device_id=peer(to), device_id_type=MESH,
             ).start()
 
     @pl.when(me == 1)
     def _():
-        clients = range(12, 16)
         tok_wait(0, 1)
         tok_wait(1, 2)
         pl.semaphore_wait(barrier, 4)
-        hub_pass(clients, 0, 4)
+        hub_pass((12, 14), 0, 0)
         tok_wait(2, 2)
-        hub_pass(clients, 4, 6)
+        hub_pass(range(12, 16), 4, 1)
         tok_wait(3, 2)
-        hub_pass(clients, 6, 8)
+        hub_pass(range(12, 16), 6, 1)
 
     @pl.when(me == 5)
     def _():
-        clients = (8, 9)
         tok_wait(2, 1)
         tok_wait(1, 2)
         pl.semaphore_wait(barrier, 2)
-        hub_pass(clients, 2, 6)
+        hub_pass((8,), 2, 0)
         tok_wait(3, 2)
-        hub_pass(clients, 6, 8)
+        hub_pass((8, 9), 6, 1)
         tok_wait(0, 2)
-        hub_pass(clients, 0, 2)
+        hub_pass((8, 9), 0, 1)
 
     @pl.when(me == 7)
     def _():
-        clients = (10, 11)
         tok_wait(3, 1)
         tok_wait(2, 2)
         pl.semaphore_wait(barrier, 2)
-        hub_pass(clients, 4, 8)
+        hub_pass((10,), 4, 0)
         tok_wait(1, 2)
-        hub_pass(clients, 2, 4)
+        hub_pass((10, 11), 2, 1)
         tok_wait(0, 2)
-        hub_pass(clients, 0, 2)
+        hub_pass((10, 11), 0, 1)
 
     @pl.when(early & (first_core | (me == 3)))
     def _():
@@ -378,23 +391,38 @@
             def _():
                 tok_wait(chip, 2)
 
+    @pl.when(jnp.logical_not(early) & first_core)
+    def _():
+        tok_wait(1, 4)
+        slabs = tok_all.at[pl.ds(jnp.where(me < 10, 2, jnp.where(me < 12, 4, 0)), 4)]
+        pltpu.make_async_remote_copy(
+            src_ref=slabs, dst_ref=slabs, send_sem=hub_send, recv_sem=tok_recv.at[0], device_id=peer(me + 1), device_id_type=MESH
+        ).start()
+
     @pl.when(jnp.logical_not(early))
     def _():
+        tok_wait(4, NF - 1)
+        patches(1, tok_all, place, xp)
+        convolve_own(xp, now, own)
+
+    @pl.when(jnp.logical_not(early) & first_core)
+    def _():
+        tok_wait(0, 4)
+
+    @pl.when(jnp.logical_not(early | first_core))
+    def _():
         tok_wait(0, NF)
 
     patches(0, tok_all, place, xp)
-    convolve(0, xp, ft, ft0, ghalf, wcat, hid, prod)
+    convolve(0, xp, now, back, own, ghalf, wcat, hid, prod)
 
     @pl.when(early)
     def _():
         tok_wait(4, NF)
-
-    @pl.when(jnp.logical_not(early))
-    def _():
-        tok_wait(4, NF - 1)
-
-    patches(1, tok_all, place, xp)
-    convolve(1, xp, ft, ft0, ghalf, wcat, hid, prod, lambda: finish(0))
+        patches(1, tok_all, place, xp)
+        convolve_own(xp, now, own)
+
+    convolve(1, xp, now, back, own, ghalf, wcat, hid, prod, lambda: finish(0))
     finish(1)
 
     def tok_sent(count, sem):
@@ -413,12 +441,16 @@
 
     @pl.when(me == 1)
     def _():
-        tok_sent(N, hub_send)
-        tok_sent(N, hub_send)
+        tok_sent(12, hub_send)
+        tok_sent(12, hub_send)
 
     @pl.when((me == 5) | (me == 7))
     def _():
-        tok_sent(N, hub_send)
+        tok_sent(12, hub_send)
+
+    @pl.when(jnp.logical_not(early) & first_core)
+    def _():
+        tok_sent(4, hub_send)
 
     for f, (send, recv) in enumerate(((send0, recv0), (send1, recv1))):
         out_copy(f, send.at[pl.ds(0, N - 1)], recv.at[pl.ds(0, N - 1)], after).wait()
@@ -440,13 +472,14 @@
             pltpu.VMEM((1, C2), F32),
             pltpu.VMEM((HALF, 128), BF16),
             pltpu.VMEM((N, HALF, 128), BF16),
-            pltpu.VMEM((C2, 304), BF16),
             pltpu.VMEM((C2, 160), BF16),
+            pltpu.VMEM((C2, 144), BF16),
             pltpu.VMEM((C2, 128), F32),
             pltpu.VMEM((C2, 128), F32),
             pltpu.VMEM((2, 8 * HALF, FL), BF16),
             pltpu.VMEM((9 * CO, 2 * C2), BF16),
-            pltpu.VMEM((304, 4 * FL), BF16),
+            pltpu.VMEM((320, 4 * FL), BF16),
+            pltpu.VMEM((C2, 4 * FL), F32),
             pltpu.VMEM((2 * C2, 4 * FL), BF16),
             pltpu.VMEM((FR, 9 * CO, 4 * FL), F32),
             pltpu.VMEM((FR, TILES, CO, 128), F32),

time: 26.7 us -> 26.1 us (0.978)
  Pallas kernels: 26.6 us -> 25.9 us
    pallas_call x1, Pallas kernels: 25.6 us -> 24.9 us  [exchange(): pl.pallas_call(main_kernel, out_shape=(pltpu.VMEM((N, CO, 128), BF16), pl...]
where the time goes in v7:
time: 26.1 us; the launch traced here: 25.9 us
  Pallas kernels  25.9 us (99%)
    pallas_call x1, Pallas kernels, exchange(): pl.pallas_call(main_kernel, out_shape=(pltpu.VMEM((N, CO, 128), BF16), pl...  24.9 us
    pallas_call x1, Pallas kernels, assemble(): pl.pallas_call(assemble_kernel, out_shape=jax.ShapeDtypeStruct((1, FR, 9,...  0.99 us

profile of v7, /device:TPU:1, one launch (start us, length us, event | category | flops | bytes accessed | tf_op | source)
XLA Modules:
  0.0 25.9 jit_solution(16644502078753963643)
XLA Ops:
  0.0 24.9 %shard_map.73 = (bf16[16,24,128]{2,1,0:T(8,128)(2,1)S(1)}, bf16[16,32,128]{2,1,0:T(8,128)(2,1)S(1)}, bf16[144,256]{1,0:T(8,128)(2,1)S(1)}) custom-call(s32[16]{0:T(128)} %rows_ref.1, bf16[45,64]{1,0:T(8,128)(2,1)} %tok_ref.1, bf16[3,144,384]{2,1,0:T(8,128)(2,1)} %bitcast.5, f32[384]{0:T(512)} %b1_ref.1, f32[384]{0:T(512)} %gain_ref.1, ...), custom_call_target="tpu_custom_call" | custom-call | tf_op jit(solution)/shard_map/pallas_call | solution.py:461
  24.9 1.0 %shard_map.74 = bf16[1,2,9,16,384]{4,3,2,1,0:T(8,128)(2,1)} custom-call(bf16[144,256]{1,0:T(8,128)(2,1)S(1)} %get-tuple-element.8.pick, bf16[16,24,128]{2,1,0:T(8,128)(2,1)S(1)} %get-tuple-element.9.recv0, bf16[16,32,128]{2,1,0:T(8,128)(2,1)S(1)} %get-tuple-element.10.recv1), custom_call_target="tpu_custom_call" | custom-call | tf_op jit(solution)/shard_map/pallas_call | solution.py:523

commit v8 on v7

--- a/solution.py
+++ b/solution.py
@@ -136,11 +136,11 @@
     ready = first_of(ats[0])
     for n, at in enumerate(ats):
         ahead = first_of(ats[n + 1]) if n + 1 < len(ats) else None
+        if between is not None and n == 0:
+            between()
         act(at, ready)
         if n:
             second_of(ats[n - 1])
-        if between is not None and n == 1:
-            between()
         ready = ahead
     second_of(ats[-1])
 
@@ -293,8 +293,8 @@
     @pl.when(jnp.logical_not(early))
     def _():
         pl.semaphore_wait(barrier, N - 1)
+        for_others(me, 0, NF, lambda i: tok_copy(i).start())
         for_others(me, NF, N, lambda i: tok_copy(i).start())
-        for_others(me, 0, NF, lambda i: tok_copy(i).start())
 
     for copy in copies:
         copy.wait()

time: 26.1 us -> 25.8 us (0.989)
  no operation moved by 1% of the time
where the time goes in v8:
time: 25.8 us; the launch traced here: 25.7 us
  Pallas kernels  25.7 us (100%)
    pallas_call x1, Pallas kernels, exchange(): pl.pallas_call(main_kernel, out_shape=(pltpu.VMEM((N, CO, 128), BF16), pl...  24.7 us
    pallas_call x1, Pallas kernels, assemble(): pl.pallas_call(assemble_kernel, out_shape=jax.ShapeDtypeStruct((1, FR, 9,...  0.99 us

profile of v8, /device:TPU:1, one launch (start us, length us, event | category | flops | bytes accessed | tf_op | source)
XLA Modules:
  0.0 25.7 jit_solution(17821317023090455481)
XLA Ops:
  0.0 24.7 %shard_map.73 = (bf16[16,24,128]{2,1,0:T(8,128)(2,1)S(1)}, bf16[16,32,128]{2,1,0:T(8,128)(2,1)S(1)}, bf16[144,256]{1,0:T(8,128)(2,1)S(1)}) custom-call(s32[16]{0:T(128)} %rows_ref.1, bf16[45,64]{1,0:T(8,128)(2,1)} %tok_ref.1, bf16[3,144,384]{2,1,0:T(8,128)(2,1)} %bitcast.5, f32[384]{0:T(512)} %b1_ref.1, f32[384]{0:T(512)} %gain_ref.1, ...), custom_call_target="tpu_custom_call" | custom-call | tf_op jit(solution)/shard_map/pallas_call | solution.py:461
  24.7 1.0 %shard_map.74 = bf16[1,2,9,16,384]{4,3,2,1,0:T(8,128)(2,1)} custom-call(bf16[144,256]{1,0:T(8,128)(2,1)S(1)} %get-tuple-element.8.pick, bf16[16,24,128]{2,1,0:T(8,128)(2,1)S(1)} %get-tuple-element.9.recv0, bf16[16,32,128]{2,1,0:T(8,128)(2,1)S(1)} %get-tuple-element.10.recv1), custom_call_target="tpu_custom_call" | custom-call | tf_op jit(solution)/shard_map/pallas_call | solution.py:523

commit v9 on v8

--- a/solution.py
+++ b/solution.py
@@ -352,11 +352,11 @@
         tok_wait(0, 1)
         tok_wait(1, 2)
         pl.semaphore_wait(barrier, 4)
-        hub_pass((12, 14), 0, 0)
+        hub_pass((14, 12), 0, 0)
         tok_wait(2, 2)
-        hub_pass(range(12, 16), 4, 1)
+        hub_pass((14, 15, 12, 13), 4, 1)
         tok_wait(3, 2)
-        hub_pass(range(12, 16), 6, 1)
+        hub_pass((14, 15, 12, 13), 6, 1)
 
     @pl.when(me == 5)
     def _():

time: 25.8 us -> 25.5 us (0.988)
  Pallas kernels: 25.7 us -> 25.4 us
    pallas_call x1, Pallas kernels: 24.7 us -> 24.4 us  [exchange(): pl.pallas_call(main_kernel, out_shape=(pltpu.VMEM((N, CO, 128), BF16), pl...]
where the time goes in v9:
time: 25.5 us; the launch traced here: 25.4 us
  Pallas kernels  25.4 us (100%)
    pallas_call x1, Pallas kernels, exchange(): pl.pallas_call(main_kernel, out_shape=(pltpu.VMEM((N, CO, 128), BF16), pl...  24.4 us
    pallas_call x1, Pallas kernels, assemble(): pl.pallas_call(assemble_kernel, out_shape=jax.ShapeDtypeStruct((1, FR, 9,...  0.99 us

profile of v9, /device:TPU:1, one launch (start us, length us, event | category | flops | bytes accessed | tf_op | source)
XLA Modules:
  0.0 25.4 jit_solution(14636348348905382991)
XLA Ops:
  0.0 24.4 %shard_map.73 = (bf16[16,24,128]{2,1,0:T(8,128)(2,1)S(1)}, bf16[16,32,128]{2,1,0:T(8,128)(2,1)S(1)}, bf16[144,256]{1,0:T(8,128)(2,1)S(1)}) custom-call(s32[16]{0:T(128)} %rows_ref.1, bf16[45,64]{1,0:T(8,128)(2,1)} %tok_ref.1, bf16[3,144,384]{2,1,0:T(8,128)(2,1)} %bitcast.5, f32[384]{0:T(512)} %b1_ref.1, f32[384]{0:T(512)} %gain_ref.1, ...), custom_call_target="tpu_custom_call" | custom-call | tf_op jit(solution)/shard_map/pallas_call | solution.py:461
  24.4 1.0 %shard_map.74 = bf16[1,2,9,16,384]{4,3,2,1,0:T(8,128)(2,1)} custom-call(bf16[144,256]{1,0:T(8,128)(2,1)S(1)} %get-tuple-element.8.pick, bf16[16,24,128]{2,1,0:T(8,128)(2,1)S(1)} %get-tuple-element.9.recv0, bf16[16,32,128]{2,1,0:T(8,128)(2,1)S(1)} %get-tuple-element.10.recv1), custom_call_target="tpu_custom_call" | custom-call | tf_op jit(solution)/shard_map/pallas_call | solution.py:523
